TPU v7x, 512 devices: a whole 4x4x16 slice. The times are simulated.
512 devices in a mesh: turn: 8 (over x, core), river: 16 (over z), bucket: 4 (over y).
Axes of the slice: x: 4, y: 4, z: 16, core: 2. Of those that a mesh axis runs over, the one named last changes fastest.
Arguments:
- reach_in: float32 [8, 32, 1326], P('turn', 'river'), may hold values from 0.05 to 1
- hand_live: int32 [8, 32, 1326], P('turn', 'river'), may hold values 0 or 1
- hand_rank: int32 [8, 32, 1326], P('turn', 'river'), may hold values from 0 to 4095
- hand_bucket: int32 [8, 32, 1326], P('turn', 'river'), may hold values from 0 to 8959, as said below
- strategy: bfloat16 [8960, 384], P(('river', 'bucket')), may hold values from 0.049804688 to 1
- line_acts: int32 [512, 4], P('bucket'), may hold values from 0 to 384
- line_kind: int32 [512], P('bucket'), may hold values from 0 to 2
- line_pot: float32 [512], P('bucket'), may hold values from 2 to 24
Outputs:
- river_value: float32 [8, 32, 32, 1326], P('turn', 'river', 'bucket')
- turn_value: float32 [8, 32, 1326], P('turn', 'bucket')
- flop_value: float32 [32, 1326], P('bucket')
Inputs may be any that keep to these rules, and one draw needn't show every extreme that they name: `hand_bucket`: on every board at most 64 hands have buckets in one device's block of 8960 / (river times bucket devices) consecutive table rows, and exactly 64 in some blocks of every board.
All inputs are finite; a program needn't handle non-finite values. No bound on the sum of `hand_live` on one device may be relied on, other than what follows from the above.
Results may differ from a plain program's by a relative error of at most 0.0003.
Values may be sent and summed in bfloat16 or wider, within the bound.
No kernel may reach another device: no remote copies, remote signals or barrier semaphores. Data moves between devices by JAX's collectives and lax.ppermute only.
A program may use at most 64 MiB of HBM per device.

v0:
```python
import jax
import jax.numpy as jnp
import numpy as np
from jax import lax
from jax.sharding import PartitionSpec as P

OPTIONS = 2
REPLIES = 8


def card_table(count):
    upper_card, lower_card = np.triu_indices(52, 1)
    return (
        jnp.asarray(upper_card[:count].astype(np.int32)),
        jnp.asarray(lower_card[:count].astype(np.int32)),
    )


def pair_tables(
    rank_rows, live_rows, rank_cols, live_cols, upper_rows, lower_rows, upper_cols, lower_cols
):
    clashes = (upper_rows[:, None] == upper_cols[None, :]) | (
        upper_rows[:, None] == lower_cols[None, :]
    )
    clashes = (
        clashes
        | (lower_rows[:, None] == upper_cols[None, :])
        | (lower_rows[:, None] == lower_cols[None, :])
    )
    usable = jnp.logical_not(clashes) & (live_rows[:, None] > 0) & (live_cols[None, :] > 0)
    contest = jnp.where(usable, jnp.sign(rank_rows[:, None] - rank_cols[None, :]), 0)
    return (contest.astype(jnp.bfloat16), usable.astype(jnp.bfloat16))


def fetch_rows(asked_ids, strategy):
    return lax.all_to_all(
        strategy[
            lax.all_to_all(asked_ids, ("river", "bucket"), split_axis=0, concat_axis=0, tiled=True)
        ],
        ("river", "bucket"),
        split_axis=0,
        concat_axis=0,
        tiled=True,
    )


def build_requests(owner_index, board_index, local_row, owners, boards, capacity):
    owner_marks = (owner_index[:, :, None] == jnp.arange(owners)[None, None, :]).astype(jnp.int32)
    slot_index = jnp.sum(jnp.cumsum(owner_marks, axis=1) * owner_marks, axis=2) - 1
    request = (
        jnp.zeros((owners, boards, capacity), jnp.int32)
        .at[owner_index, board_index, slot_index]
        .set(local_row)
    )
    return (request, slot_index)


def local(reach_in, hand_live, hand_rank, hand_bucket, strategy, line_acts, line_kind, line_pot):
    turns_here, rivers_here, hand_count = reach_in.shape
    boards = turns_here * rivers_here
    row_width = strategy.shape[1]
    shard_rows = strategy.shape[0]
    line_count = line_acts.shape[0]
    depth_count = line_acts.shape[1]
    group_size = lax.axis_size("bucket")
    river_count = lax.axis_size("river")
    owners = river_count * group_size
    capacity = group_size * ((3 * hand_count + owners * group_size - 1) // (owners * group_size))
    bucket_flat = hand_bucket.reshape(boards, hand_count)
    owner_index = bucket_flat // shard_rows
    local_row = bucket_flat % shard_rows
    board_index = jnp.broadcast_to(jnp.arange(boards)[:, None], (boards, hand_count))
    reach_flat = reach_in.reshape(boards, hand_count) * hand_live.reshape(
        boards, hand_count
    ).astype(jnp.float32)
    act_index = jnp.arange(row_width)
    request, slot_index = build_requests(
        owner_index, board_index, local_row, owners, boards, capacity
    )
    gathered_rows = fetch_rows(request, strategy)
    picks = (line_acts.T[:, None, :] == act_index[None, :, None]).astype(jnp.bfloat16)
    absent = (line_acts.T == row_width).astype(jnp.float32)

    def one_board(inputs):
        rows_board, reach_row = inputs
        product = reach_row[:, None]
        for depth_index in range(depth_count):
            looked = jnp.dot(rows_board, picks[depth_index], preferred_element_type=jnp.float32)
            product = product * (looked + absent[depth_index][None, :])
        return product.astype(jnp.bfloat16)

    reach_lines = lax.map(
        one_board, (gathered_rows[owner_index, board_index, slot_index], reach_flat)
    )
    upper_card, lower_card = card_table(hand_count)
    payoff_sign = jnp.where(line_kind == 1, 1.0, jnp.where(line_kind == 2, -1.0, 0.0)).astype(
        jnp.float32
    )
    showdown_line = line_kind == 0
    scale_line = line_pot / hand_count
    block_count = 6
    block_rows = hand_count // block_count
    entries_here = line_count // (OPTIONS * REPLIES)

    def board_value(inputs):
        reach_line, live_row, rank_row = inputs

        def block_value(block_inputs):
            rank_block, live_block, upper_block, lower_block = block_inputs
            contest, usable = pair_tables(
                rank_block,
                live_block,
                rank_row,
                live_row,
                upper_block,
                lower_block,
                upper_card,
                lower_card,
            )
            showdown = jnp.dot(contest, reach_line, preferred_element_type=jnp.float32)
            folded = jnp.dot(usable, reach_line, preferred_element_type=jnp.float32)
            return (
                jnp.where(showdown_line[None, :], showdown, payoff_sign[None, :] * folded)
                * scale_line[None, :]
            )

        block_inputs = (
            rank_row.reshape(block_count, block_rows),
            live_row.reshape(block_count, block_rows),
            upper_card.reshape(block_count, block_rows),
            lower_card.reshape(block_count, block_rows),
        )
        values = lax.map(block_value, block_inputs).reshape(hand_count, -1)
        best_value = jnp.max(
            jnp.sum(values.reshape(hand_count, entries_here, OPTIONS, REPLIES), axis=3), axis=2
        )
        return best_value.T

    board_inputs = (
        reach_lines,
        hand_live.reshape(boards, hand_count),
        hand_rank.reshape(boards, hand_count),
    )
    river_value = lax.map(board_value, board_inputs).reshape(
        turns_here, rivers_here, entries_here, hand_count
    )
    rivers_total = rivers_here * lax.axis_size("river")
    turns_total = turns_here * lax.axis_size("turn")
    turn_value = lax.psum(jnp.sum(river_value, axis=1), "river") / rivers_total
    flop_value = lax.psum(jnp.sum(turn_value, axis=0), "turn") / turns_total
    return (river_value, turn_value, flop_value)


def solution(mesh):
    return jax.shard_map(
        local,
        mesh=mesh,
        in_specs=(
            P("turn", "river", None),
            P("turn", "river", None),
            P("turn", "river", None),
            P("turn", "river", None),
            P(("river", "bucket"), None),
            P("bucket", None),
            P("bucket"),
            P("bucket"),
        ),
        out_specs=(
            P("turn", "river", "bucket", None),
            P("turn", "bucket", None),
            P("bucket", None),
        ),
        check_vma=False,
    )
```

profile of v0, /device:TPU:1, one launch (start us, length us, event | category | flops | bytes accessed | tf_op | source)
XLA Modules:
  0.0 580.7 jit_solution(10341422330768187699)
XLA Ops:
  0.6 0.8 and_select_fusion
  1.7 36.3 %reduce-window.6 = s32[2,64,11,128]{3,2,1,0:T(8,128)S(1)} reduce-window(s32[2,64,11,128]{3,2,1,0:T(8,128)S(1)} %reshape.207, s32[]{:T(128)} %constant.59.clone.1), window={size=1x1x1x128 pad=0_0x0_0x0_0x127_0}, to_apply=%region_0.1 | reduce-window | flops 22888448 | bytes 1441796 | tf_op jit(solution)/shard_map/reduce-window
  40.4 13.5 %scatter_custom_fusion = s32[8192]{0:T(1024)S(1)} fusion(s32[2652]{0:T(1024)S(1)} %reshape.222, s32[2652]{0:T(1024)S(1)} %reshape.224, s32[]{:T(128)} %constant.59.clone.1), kind=kCustom, calls=%fused_computation.82 | custom fusion | bytes 32772
  54.2 32.5 %all_to_all.10 = s32[64,1,128]{2,1,0:T(1,128)S(1)} all-to-all(s32[64,1,128]{2,1,0:T(1,128)S(1)} %reshape.238), channel_id=1, replica_groups=mesh['turn'=8,'river'=16,'bucket'=4] {'river','bucket'}, dimensions={0} | all-to-all | bytes 65536 | tf_op jit(solution)/shard_map/all_to_all | solution.py:38
  87.2 0.7 reduce.16
  88.2 33.2 %gather_fusion = bf16[8192,384]{1,0:T(8,128)(2,1)} fusion(bf16[140,384]{1,0:T(8,128)(2,1)S(1)} %copy-done, s32[8192]{0:T(1024)S(1)} %broadcast_clamp_fusion), kind=kCustom, calls=%fused_computation | custom fusion | bytes 12615680 | tf_op jit(solution)/shard_map/gather | solution.py:37
  121.4 6.0 %all-to-all-start.1 = ((bf16[64,2,64,384]{3,2,1,0:T(8,128)(2,1)}), bf16[64,2,64,384]{3,2,1,0:T(8,128)(2,1)}, u32[]{:S(2)}, u32[]{:S(2)}) async-start(bf16[64,2,64,384]{3,2,1,0:T(8,128)(2,1)} %bitcast.133), calls=%async_computation.1 | async-start | bytes 12582912 | tf_op jit(solution)/shard_map/all_to_all | solution.py:36
  127.7 273.0 %all-to-all-done.1 = bf16[64,2,64,384]{3,2,1,0:T(8,128)(2,1)} async-done(((bf16[64,2,64,384]{3,2,1,0:T(8,128)(2,1)}), bf16[64,2,64,384]{3,2,1,0:T(8,128)(2,1)}, u32[]{:S(2)}, u32[]{:S(2)}) %all-to-all-start.1) | async-done | bytes 6291488 | tf_op jit(solution)/shard_map/all_to_all | solution.py:36
  400.8 52.1 %gather_fusion.1 = bf16[2652,384]{1,0:T(8,128)(2,1)} fusion(bf16[64,2,64,384]{3,2,1,0:T(8,128)(2,1)} %all-to-all-done.1, s32[2652]{0:T(1024)S(1)} %reshape.216), kind=kCustom, calls=%fused_computation.1 | custom fusion | bytes 4105296 | tf_op jit(solution)/shard_map/gather | solution.py:93
  452.9 2.0 reshape.219
  454.9 4.6 while.34
  459.5 39.0 %while.36 = (s32[]{:T(128)}, f32[2,8,1326]{2,1,0:T(8,128)S(1)}, s32[2,1326]{1,0:T(2,128)S(1)}, s32[2,1326]{1,0:T(2,128)S(1)}, bf16[2,1326,128]{2,1,0:T(8,128)(2,...) while((s32[]{:T(128)}, f32[2,8,1326]{2,1,0:T(8,128)S(1)}, ...), condition=%wide.region_11.12_spmd.clone, body=%wide.region_6.11_spmd.sunk.clone.sunk | while | flops 157318192 | bytes 5496284 | solution.py:144
  459.8 18.0 %while.37 = (s32[]{:T(128)}, f32[6,221,128]{2,1,0:T(8,128)S(1)}, pred[128]{0:T(512)(128)(4,1)S(1)}, s32[6,221]{1,0:T(8,128)}, s32[6,221]{1,0:T(8,128)}, /*index=...) while((s32[]{:T(128)}, f32[6,221,128]{2,1,0:T(8,128)S(1)}, ...), condition=%wide.region_8.8_spmd.clone, body=%wide.region_7.7_spmd.sunk.clone.sunk | while | flops 157159072 | bytes 1077787 | solution.py:133
  459.8 0.7 constant_dynamic-slice_fusion.6
  460.5 0.7 constant_dynamic-slice_fusion.7
  461.2 0.8 fusion.76
  462.8 0.7 constant_dynamic-slice_fusion.6
  463.5 0.7 constant_dynamic-slice_fusion.7
  464.3 0.8 fusion.76
  465.8 0.7 constant_dynamic-slice_fusion.6
  466.5 0.7 constant_dynamic-slice_fusion.7
  467.3 0.8 fusion.76
  468.8 0.7 constant_dynamic-slice_fusion.6
  469.5 0.7 constant_dynamic-slice_fusion.7
  470.3 0.8 fusion.76
  471.8 0.7 constant_dynamic-slice_fusion.6
  473.3 0.8 fusion.76
  474.8 0.7 constant_dynamic-slice_fusion.6
  476.3 0.8 fusion.76
  479.3 18.0 %while.37 = (s32[]{:T(128)}, f32[6,221,128]{2,1,0:T(8,128)S(1)}, pred[128]{0:T(512)(128)(4,1)S(1)}, s32[6,221]{1,0:T(8,128)}, s32[6,221]{1,0:T(8,128)}, /*index=...) while((s32[]{:T(128)}, f32[6,221,128]{2,1,0:T(8,128)S(1)}, ...), condition=%wide.region_8.8_spmd.clone, body=%wide.region_7.7_spmd.sunk.clone.sunk | while | flops 157159072 | bytes 1077787 | solution.py:133
  479.3 0.7 constant_dynamic-slice_fusion.6
  480.0 0.7 constant_dynamic-slice_fusion.7
  480.8 0.8 fusion.76
  482.3 0.7 constant_dynamic-slice_fusion.6
  483.0 0.7 constant_dynamic-slice_fusion.7
  483.8 0.8 fusion.76
  485.3 0.7 constant_dynamic-slice_fusion.6
  486.0 0.7 constant_dynamic-slice_fusion.7
  486.8 0.8 fusion.76
  488.3 0.7 constant_dynamic-slice_fusion.6
  489.0 0.7 constant_dynamic-slice_fusion.7
  489.8 0.8 fusion.76
  491.3 0.7 constant_dynamic-slice_fusion.6
  492.8 0.8 fusion.76
  494.3 0.7 constant_dynamic-slice_fusion.6
  495.8 0.8 fusion.76
  498.6 42.1 %psum.14 = f32[1,8,1326]{2,1,0:T(8,128)S(1)} all-reduce(f32[1,8,1326]{2,1,0:T(8,128)S(1)} %bitcast.140), channel_id=1, replica_groups=mesh['turn'=8,'river'=16,'bucket'=4] {'river'}, use_global_device_ids=true, to_apply=%region_13.14 | all-reduce | flops 10608 | bytes 84864 | tf_op jit(solution)/shard_map/psum | solution.py:149
  541.3 38.8 %psum.15 = f32[8,1326]{1,0:T(8,128)S(1)} all-reduce(f32[8,1326]{1,0:T(8,128)S(1)} %fusion.45), channel_id=1, replica_groups=mesh['turn'=8,'river'=16,'bucket'=4] {'turn'}, use_global_device_ids=true, to_apply=%region_14.15 | all-reduce | flops 10608 | bytes 84864 | tf_op jit(solution)/shard_map/psum | solution.py:150
  (135 shorter events, 23.8 us)
Async XLA Ops:
  0.6 87.6 %copy-start = (bf16[140,384]{1,0:T(8,128)(2,1)S(1)}, bf16[140,384]{1,0:T(8,128)(2,1)}, u32[]{:S(2)}) copy-start(bf16[140,384]{1,0:T(8,128)(2,1)} %param.20) | copy-start | bytes 322564
  39.2 0.7 copy-start.4
  39.2 0.8 copy-start.8
  39.3 0.9 copy-start.7
  121.4 6.1 %copy-start.9 = (s32[128]{0:T(128)S(1)}, s32[128]{0:T(128)}, u32[]{:S(2)}) copy-start(s32[128]{0:T(128)} %param.22) | copy-start | bytes 1540
  121.4 6.2 %copy-start.10 = (f32[128]{0:T(128)S(1)}, f32[128]{0:T(128)}, u32[]{:S(2)}) copy-start(f32[128]{0:T(128)} %param.23) | copy-start | bytes 1540
  121.4 6.2 %copy-start.6 = (s32[128,4]{0,1:T(4,128)S(1)}, s32[128,4]{0,1:T(4,128)}, u32[]{:S(2)}) copy-start(s32[128,4]{0,1:T(4,128)} %param.21) | copy-start | bytes 6148
  121.4 6.3 %copy-start.1 = (s32[1,2,1326]{2,1,0:T(2,128)S(1)}, s32[1,2,1326]{2,1,0:T(2,128)}, u32[]{:S(2)}) copy-start(s32[1,2,1326]{2,1,0:T(2,128)} %param.17) | copy-start | bytes 31828
  121.4 6.3 %copy-start.5 = (f32[1,2,1326]{2,1,0:T(2,128)S(1)}, f32[1,2,1326]{2,1,0:T(2,128)}, u32[]{:S(2)}) copy-start(f32[1,2,1326]{2,1,0:T(2,128)} %param.16) | copy-start | bytes 31828
  121.4 279.3 %all-to-all-start.1 = ((bf16[64,2,64,384]{3,2,1,0:T(8,128)(2,1)}), bf16[64,2,64,384]{3,2,1,0:T(8,128)(2,1)}, u32[]{:S(2)}, u32[]{:S(2)}) async-start(bf16[64,2,64,384]{3,2,1,0:T(8,128)(2,1)} %bitcast.133), calls=%async_computation.1 | async-start | bytes 12582912 | tf_op jit(solution)/shard_map/all_to_all | solution.py:36
  454.8 4.7 copy-start.3
  454.9 4.7 copy-start.11
  454.9 4.7 copy-start.12
  498.5 82.2 %copy-start.2 = (f32[2,8,1326]{2,1,0:T(8,128)}, f32[2,8,1326]{2,1,0:T(8,128)S(1)}, u32[]{:S(2)}) copy-start(f32[2,8,1326]{2,1,0:T(8,128)S(1)} %get-tuple-element.647) | copy-start | bytes 254596
where the time goes:
time: 583 us; the launch traced here: 581 us
  waiting for transfers between devices  273 us (47%)
  local copies, waits for them, and re-layouts  123 us (21%)
  blocking collectives  113 us (19%)
  other arithmetic  41.1 us (7%)
  matrix products  22.8 us (4%)
  starting transfers between devices  6.01 us (1%)
    all_to_all x1, waiting for transfers between devices, fetch_rows(): lax.all_to_all(strategy[lax.all_to_all(asked_ids, ('river', 'bucket'), sp...  273 us
    gather x2, local copies, waits for them, and re-layouts, local(): gathered_rows[owner_index, board_index, slot_index]  54.1 us
    psum x1, blocking collectives, local(): turn_value = lax.psum(jnp.sum(river_value, axis=1), 'river') / rivers_total  42.1 us
    psum x1, blocking collectives, local(): flop_value = lax.psum(jnp.sum(turn_value, axis=0), 'turn') / turns_total  38.8 us
    another operation x6, other arithmetic  36.7 us
    gather x1, local copies, waits for them, and re-layouts, fetch_rows(): strategy[lax.all_to_all(asked_ids, ('river', 'bucket'), split_axis=0, con...  33.2 us
    all_to_all x1, blocking collectives, fetch_rows(): lax.all_to_all(asked_ids, ('river', 'bucket'), split_axis=0, concat_axis=...  32.5 us
    dynamic_slice x24, local copies, waits for them, and re-layouts, board_value(): values = lax.map(block_value, block_inputs).reshape(hand_count, -1)  16.9 us
  transfers between devices with their start and end apart: 1, of which 1 were waited for; matrix products, arithmetic and copies ran while one was open for 0% of the time, Pallas kernels for 0%

commit v1 on v0

v1 whole, which is shorter than its diff:
```python
import functools

import jax
import jax.numpy as jnp
import numpy as np
from jax import lax
from jax.experimental import pallas as pl
from jax.experimental.pallas import tpu as pltpu
from jax.sharding import PartitionSpec as P

OPTIONS = 2
REPLIES = 8
LANES = 128
CORES = 2
F32 = jnp.float32
BF16 = jnp.bfloat16


def no_clash_table(count, padded):
    upper, lower = np.triu_indices(52, 1)
    upper, lower = upper[:count], lower[:count]
    clash = (upper[:, None] == upper) | (upper[:, None] == lower)
    clash |= (lower[:, None] == upper) | (lower[:, None] == lower)
    table = np.zeros((padded, padded), np.float32)
    table[:count, :count] = ~clash
    return jnp.asarray(table, BF16)


def split_two(x):
    high = x.astype(BF16)
    return high, (x - high.astype(F32)).astype(BF16)


def split_three(x):
    high = x.astype(BF16)
    rest = x - high.astype(F32)
    middle = rest.astype(BF16)
    return high, middle, (rest - middle.astype(F32)).astype(BF16)


def dot_rows(a, b):
    return lax.dot_general(a, b, (((1,), (1,)), ((), ())), preferred_element_type=F32)


def line_sum_kernel(hand_count, rows_ref, acts_ref, kind_ref, pot_ref, sums_ref):
    blocks, rows, width = rows_ref.shape
    lines = acts_ref.shape[0]
    entries = lines // (OPTIONS * REPLIES)
    table = rows_ref[...].reshape(blocks * rows, width)
    column = lax.broadcasted_iota(jnp.int32, (lines, width), 1)
    product = None
    for depth in range(acts_ref.shape[1]):
        picks = (acts_ref[:, depth : depth + 1] == column).astype(F32).astype(BF16)
        looked = dot_rows(table, picks)
        present = dot_rows(jnp.ones((8, width), BF16), picks)
        looked = looked + (1.0 - present[0:1])
        product = looked if product is None else product * looked
    kind = kind_ref[...]
    scale = pot_ref[...] / hand_count
    sign = jnp.where(kind == 1, 1.0, jnp.where(kind == 2, -1.0, 0.0))
    weights = (jnp.where(kind == 0, scale, 0.0), sign * scale)
    line = lax.broadcasted_iota(jnp.int32, (lines, LANES), 0)
    lane = lax.broadcasted_iota(jnp.int32, (lines, LANES), 1)
    slot = ((line // REPLIES) % OPTIONS) * entries + line // (REPLIES * OPTIONS)
    group = OPTIONS * entries
    total = jnp.zeros((rows, LANES), F32)
    for kind_index, weight in enumerate(weights):
        pieces = split_three(product * weight)
        for block in range(blocks):
            target = slot + (block * 2 + kind_index) * group
            gather = (lane == target).astype(F32).astype(BF16)
            for piece in pieces:
                total += jnp.dot(
                    piece[block * rows : (block + 1) * rows],
                    gather,
                    preferred_element_type=F32,
                )
    sums_ref[...] = total


def board_kernel(
    shard_rows, half_rows, blocks, core_ref, mine_ref, other_ref, reach_ref, live_ref, rank_ref,
    rank_col_ref, bucket_ref, table_ref, river_ref, part_ref, sums_ref, index_ref, group_ref,
    reach_scratch, rank_scratch, show_ref, fold_ref, contest_ref,
):
    boards, hands = reach_ref.shape
    padded = table_ref.shape[0]
    wide = index_ref.shape[1]
    held = mine_ref.shape[0]
    slots = 2 * held
    core = core_ref[0, 0]

    for part, ref in enumerate((mine_ref, other_ref)):
        for start in range(0, held, LANES):
            high, low = split_two(ref[start : start + LANES, :].T)
            at = part * held + start
            sums_ref[0:LANES, at : at + LANES] = high
            sums_ref[LANES : 2 * LANES, at : at + LANES] = low

    bucket = bucket_ref[...].astype(F32)
    owner = jnp.floor((bucket + 0.5) * (1.0 / shard_rows))
    row = bucket - owner * shard_rows
    place = jnp.floor((owner + 0.5) * (1.0 / blocks))
    block = owner - place * blocks
    half = jnp.where(row >= half_rows, 1.0, 0.0)
    row = row - half * (shard_rows - half_rows)
    elsewhere = jnp.where(half == core.astype(F32), 0.0, 1.0)
    index = elsewhere * held + place * half_rows + row
    index_ref[...] = jnp.full(index_ref.shape, -1, jnp.int32)
    group_ref[...] = jnp.zeros(group_ref.shape, F32)
    reach_scratch[...] = jnp.zeros(reach_scratch.shape, F32)
    rank_scratch[...] = jnp.zeros(rank_scratch.shape, F32)
    index_ref[0:boards, 0:hands] = index.astype(jnp.int32)
    group_ref[0:boards, 0:hands] = block
    reach_scratch[0:boards, 0:hands] = reach_ref[...] * live_ref[...].astype(F32)
    rank_scratch[0:boards, 0:hands] = rank_ref[...].astype(F32)

    step = 2 * LANES
    columns = LANES // blocks
    half_columns = columns // 2

    for board in range(boards):

        def gather(turn, carry, board=board):
            start = pl.multiple_of(turn * step, step)
            lanes = pl.ds(start, step)
            index = index_ref[board : board + 1, lanes]
            position = lax.broadcasted_iota(jnp.int32, (slots, step), 0)
            marks = (position == index).astype(F32).astype(BF16)
            found = jnp.dot(sums_ref[...], marks, preferred_element_type=F32)
            found = found[0:LANES] + found[LANES : 2 * LANES]
            group = group_ref[board : board + 1, lanes]
            chosen = jnp.zeros((columns, step), F32)
            for which in range(blocks):
                chosen += jnp.where(
                    group == which, found[which * columns : (which + 1) * columns], 0.0
                )
            chosen = chosen * reach_scratch[board : board + 1, lanes]
            high, low = split_two(chosen)
            show_ref[board, 0:half_columns, lanes] = high[0:half_columns]
            show_ref[board, half_columns:columns, lanes] = low[0:half_columns]
            base = board * columns
            fold_ref[base : base + half_columns, lanes] = high[half_columns:columns]
            fold_ref[base + half_columns : base + columns, lanes] = low[half_columns:columns]
            return carry

        lax.fori_loop(0, wide // step, gather, 0)

    folded = jnp.dot(fold_ref[:, 0:padded], table_ref[...], preferred_element_type=F32)
    total = None
    for board in range(boards):

        def build(turn, carry, board=board):
            rows = pl.ds(pl.multiple_of(turn * LANES, LANES), LANES)
            rank_row = rank_scratch[board : board + 1, :]
            rank_col = rank_col_ref[rows, board : board + 1]
            order = jnp.clip(rank_row - rank_col, -1.0, 1.0)
            contest_ref[rows, :] = (order * table_ref[rows, :].astype(F32)).astype(BF16)
            return carry

        lax.fori_loop(0, padded // LANES, build, 0)
        shown = jnp.dot(show_ref[board, :, 0:padded], contest_ref[...], preferred_element_type=F32)
        base = board * columns
        value = shown[0:half_columns] + shown[half_columns:columns]
        value = value + (
            folded[base : base + half_columns] + folded[base + half_columns : base + columns]
        )
        entries = half_columns // OPTIONS
        best = jnp.maximum(value[0:entries], value[entries:half_columns])
        best = best[:, 0:hands] * live_ref[board : board + 1, :].astype(F32)
        river_ref[board] = best
        total = best if total is None else total + best
    part_ref[...] = total


def whole_vmem():
    return pl.BlockSpec(memory_space=pltpu.VMEM)


def local(reach_in, hand_live, hand_rank, hand_bucket, strategy, line_acts, line_kind, line_pot):
    turns_here, rivers_here, hands = reach_in.shape
    boards = turns_here * rivers_here
    shard_rows, width = strategy.shape
    lines = line_acts.shape[0]
    entries = lines // (OPTIONS * REPLIES)
    blocks = lax.axis_size("bucket")
    rivers = lax.axis_size("river")
    turns = lax.axis_size("turn")
    padded = -(-hands // LANES) * LANES
    wide = -(-hands // (2 * LANES)) * 2 * LANES
    half_rows = -(-shard_rows // (CORES * 8)) * 8
    core = lax.axis_index("turn") % CORES

    with jax.named_scope("share_rows"):
        part = lax.dynamic_slice_in_dim(
            strategy, core * (shard_rows - half_rows), half_rows, axis=0
        )
        rows = lax.all_to_all(
            jnp.broadcast_to(part[None], (blocks, half_rows, width)),
            "bucket",
            split_axis=0,
            concat_axis=0,
            tiled=True,
        )
    with jax.named_scope("line_sums"):
        sums = pl.pallas_call(
            functools.partial(line_sum_kernel, hands),
            out_shape=jax.ShapeDtypeStruct((half_rows, LANES), F32),
            in_specs=[whole_vmem()] * 4,
            out_specs=whole_vmem(),
            compiler_params=pltpu.CompilerParams(vmem_limit_bytes=32 * 2**20),
        )(rows, line_acts, line_kind.reshape(1, lines), line_pot.reshape(1, lines))
    with jax.named_scope("share_sums"):
        mine = lax.all_gather(sums, "river", axis=0, tiled=True)
        swap = [(device, device ^ 1) for device in range(turns)]
        other = lax.ppermute(mine, "turn", swap)
    with jax.named_scope("boards"):
        rank = hand_rank.reshape(boards, hands)
        rank_col = jnp.pad(rank.T.astype(F32), ((0, padded - hands), (0, 0)))
        slots = 2 * rivers * half_rows
        river, partial = pl.pallas_call(
            functools.partial(board_kernel, shard_rows, half_rows, blocks),
            out_shape=(
                jax.ShapeDtypeStruct((boards, entries, hands), F32),
                jax.ShapeDtypeStruct((entries, hands), F32),
            ),
            in_specs=[pl.BlockSpec(memory_space=pltpu.SMEM)] + [whole_vmem()] * 8,
            out_specs=(whole_vmem(), whole_vmem()),
            scratch_shapes=[
                pltpu.VMEM((2 * LANES, slots), BF16),
                pltpu.VMEM((8, wide), jnp.int32),
                pltpu.VMEM((8, wide), F32),
                pltpu.VMEM((8, wide), F32),
                pltpu.VMEM((8, padded), F32),
                pltpu.VMEM((boards, LANES // blocks, wide), BF16),
                pltpu.VMEM((boards * LANES // blocks, wide), BF16),
                pltpu.VMEM((padded, padded), BF16),
            ],
            compiler_params=pltpu.CompilerParams(vmem_limit_bytes=48 * 2**20),
        )(
            core.astype(jnp.int32).reshape(1, 1),
            mine,
            other,
            reach_in.reshape(boards, hands),
            hand_live.reshape(boards, hands),
            rank,
            rank_col,
            hand_bucket.reshape(boards, hands),
            no_clash_table(hands, padded),
        )
    river_value = river.reshape(turns_here, rivers_here, entries, hands)
    with jax.named_scope("means"):
        by_river = lax.all_gather(partial, "river", axis=0, tiled=False)
        turn_value = jnp.sum(by_river, axis=0) / (rivers * rivers_here)
        by_turn = lax.all_gather(turn_value, "turn", axis=0, tiled=False)
        flop_value = jnp.sum(by_turn, axis=0) / (turns * turns_here)
    return river_value, turn_value[None], flop_value


def solution(mesh):
    return jax.shard_map(
        local,
        mesh=mesh,
        in_specs=(
            P("turn", "river", None),
            P("turn", "river", None),
            P("turn", "river", None),
            P("turn", "river", None),
            P(("river", "bucket"), None),
            P("bucket", None),
            P("bucket"),
            P("bucket"),
        ),
        out_specs=(
            P("turn", "river", "bucket", None),
            P("turn", "bucket", None),
            P("bucket", None),
        ),
        check_vma=False,
    )
```

time: 583 us -> 121 us (0.21)
  waiting for transfers between devices: 273 us -> 4.78 us
  local copies, waits for them, and re-layouts: 123 us -> 7.05 us
  other arithmetic: 41.1 us -> 1.39 us
  blocking collectives: 113 us -> 76.2 us
  matrix products: 22.8 us -> 0 us
  Pallas kernels: 0 us -> 14.6 us
  starting transfers between devices: 6.01 us -> 15.4 us
    all_to_all x1, waiting for transfers between devices: 273 us -> 4.52 us  [local(): lax.all_to_all(jnp.broadcast_to(part[None], (blocks, half_rows, width)),...]
    gather x3 -> x0, local copies, waits for them, and re-layouts: 87.3 us -> none  [the longest x2 54.1 us: local(): gathered_rows[owner_index, board_index, slot_index]]
    psum x2 -> x0, blocking collectives: 80.9 us -> none  [the longest x1 42.1 us: local(): turn_value = lax.psum(jnp.sum(river_value, axis=1), 'river') / rivers_total]
    all_gather x0 -> x3, blocking collectives: none -> 76.2 us  [the longest x1 32.4 us: local(): mine = lax.all_gather(sums, 'river', axis=0, tiled=True)]
    another operation x6 -> x0, other arithmetic: 36.7 us -> none
    all_to_all x1 -> x0, blocking collectives: 32.5 us -> none  [fetch_rows(): lax.all_to_all(asked_ids, ('river', 'bucket'), split_axis=0, concat_axis=...]
    dot_general x32 -> x0, matrix products: 22.8 us -> none  [the longest x12 10.1 us: block_value(): showdown = jnp.dot(contest, reach_line, preferred_element_type=jnp.float32)]
    dynamic_slice x28 -> x1, local copies, waits for them, and re-layouts: 17.1 us -> 0.02 us  [local(): lax.dynamic_slice_in_dim(strategy, core * (shard_rows - half_rows), half_...]
  transfers between devices with their start and end apart: 1 -> 2, of which waited for: 1 -> 2; matrix products, arithmetic and copies ran while one was open for 0% -> 2% of each run, Pallas kernels for 0% -> 0%
where the time goes in v1:
time: 121 us; the launch traced here: 120 us
  blocking collectives  76.2 us (63%)
  starting transfers between devices  15.4 us (13%)
  Pallas kernels  14.6 us (12%)
  local copies, waits for them, and re-layouts  7.05 us (6%)
  waiting for transfers between devices  4.78 us (4%)
  other arithmetic  1.39 us (1%)
    all_gather x1, blocking collectives, local(): mine = lax.all_gather(sums, 'river', axis=0, tiled=True)  32.4 us
    all_gather x1, blocking collectives, local(): by_river = lax.all_gather(partial, 'river', axis=0, tiled=False)  23.3 us
    all_gather x1, blocking collectives, local(): by_turn = lax.all_gather(turn_value, 'turn', axis=0, tiled=False)  20.5 us
    pallas_call x1, Pallas kernels, local(): pl.pallas_call(functools.partial(board_kernel, shard_rows, half_rows, blo...  13.2 us
    ppermute x1, starting transfers between devices, local(): other = lax.ppermute(mine, 'turn', swap)  10.4 us
    unnamed x16, local copies, waits for them, and re-layouts  6.04 us
    all_to_all x1, starting transfers between devices, local(): lax.all_to_all(jnp.broadcast_to(part[None], (blocks, half_rows, width)),...  5.01 us
    all_to_all x1, waiting for transfers between devices, local(): lax.all_to_all(jnp.broadcast_to(part[None], (blocks, half_rows, width)),...  4.52 us
  transfers between devices with their start and end apart: 2, of which 2 were waited for; matrix products, arithmetic and copies ran while one was open for 2% of the time, Pallas kernels for 0%

profile of v1, /device:TPU:1, one launch (start us, length us, event | category | flops | bytes accessed | tf_op | source)
XLA Modules:
  0.0 120.2 jit_solution(10446166495629799813)
XLA Ops:
  0.6 0.0 copy-start
  0.6 0.0 copy-start.4
  0.7 0.0 copy-start.3
  0.7 0.0 copy-start.2
  0.7 0.8 copy-done
  1.6 0.7 broadcast_in_dim.2
  2.3 5.0 %all-to-all-start = ((bf16[4,72,384]{2,1,0:T(8,128)(2,1)}), bf16[4,72,384]{2,1,0:T(8,128)(2,1)S(1)}, u32[]{:S(2)}, u32[]{:S(2)}) async-start(bf16[4,72,384]{2,1,0:T(8,128)(2,1)} %broadcast_in_dim.2), calls=%async_computation | async-start | bytes 442368 | tf_op jit(solution)/shard_map/share_rows/all_to_all | solution.py:198
  7.3 0.8 copy.12.acts_ref
  8.1 4.5 %all-to-all-done.rows_ref = bf16[4,72,384]{2,1,0:T(8,128)(2,1)S(1)} async-done(((bf16[4,72,384]{2,1,0:T(8,128)(2,1)}), bf16[4,72,384]{2,1,0:T(8,128)(2,1)S(1)}, u32[]{:S(2)}, u32[]{:S(2)}) %all-to-all-start) | async-done | bytes 221216 | tf_op jit(solution)/shard_map/share_rows/all_to_all | solution.py:198
  12.6 0.0 copy-start.5
  12.6 0.7 copy-done.5
  13.2 0.0 copy-start.6
  13.2 0.7 copy-done.6
  13.9 1.4 %line_sums.1 = f32[72,128]{1,0:T(8,128)S(1)} custom-call(bf16[4,72,384]{2,1,0:T(8,128)(2,1)S(1)} %all-to-all-done.rows_ref, s32[128,4]{1,0:T(8,128)S(1)} %copy.12.acts_ref, s32[1,128]{1,0:T(1,128)S(1)} %bitcast.20, f32[1,128]{1,0:T(1,128)S(1)} %bitcast.21), custom_call_target="tpu_custom_call" | custom-call | tf_op jit(solution)/shard_map/line_sums/pallas_call | solution.py:206
  15.3 32.4 %all_gather.13.mine_ref = f32[1152,128]{1,0:T(8,128)S(1)} all-gather(f32[72,128]{1,0:T(8,128)S(1)} %line_sums.1), channel_id=1, replica_groups=mesh['turn'=8,'river'=16,'bucket'=4] {'river'}, dimensions={0}, use_global_device_ids=true | all-gather | bytes 626688 | tf_op jit(solution)/shard_map/share_sums/all_gather | solution.py:214
  47.7 10.4 %collective-permute-start = (f32[1152,128]{1,0:T(8,128)S(1)}, f32[1152,128]{1,0:T(8,128)S(1)}, u32[]{:S(2)}, u32[]{:S(2)}) collective-permute-start(f32[1152,128]{1,0:T(8,128)S(1)} %all_gather.13.mine_ref), channel_id=1, source_target_pairs={{0,64},{64,0},{128,192},{192,128},{256,320},{320,256},{384,448},{4... | collective-permute-start | bytes 1769480 | tf_op jit(solution)/shard_map/share_sums/ppermute | solution.py:216
  58.1 1.0 copy.13
  59.1 0.2 copy.14.rank_ref
  59.4 0.1 convert_bitcast_fusion
  59.5 0.3 collective-permute-done.other_ref
  59.8 0.0 copy-done.4
  59.8 0.0 copy-done.3
  59.8 0.0 copy-done.2
  59.8 0.0 copy-start.1
  59.8 2.1 %copy-done.1 = bf16[1408,1408]{1,0:T(8,128)(2,1)S(1)} copy-done((bf16[1408,1408]{1,0:T(8,128)(2,1)S(1)}, bf16[1408,1408]{1,0:T(8,128)(2,1)}, u32[]{:S(2)}) %copy-start.1) | copy-done | bytes 3964952
  61.9 13.2 %boards.1 = (f32[2,8,1326]{2,1,0:T(8,128)}, f32[8,1326]{1,0:T(8,128)S(1)}) custom-call(s32[1,1]{1,0:T(1,128)} %bitcast.core_ref, f32[1152,128]{1,0:T(8,128)S(1)} %all_gather.13.mine_ref, f32[1152,128]{1,0:T(8,128)S(1)} %collective-permute-done.other_ref, f32[2,1326]{1,0:T(2,128)S(1)} %bitcast.17, s32[2,1326]{1,0:T(2,128)S(1)} %bitcast.18, ...), custom_call_target="tpu_custom_call" | custom-call | tf_op jit(solution)/shard_map/boards/pallas_call | solution.py:221
  75.1 23.3 %all-gather = f32[128,1326]{1,0:T(8,128)S(1)} all-gather(f32[8,1326]{1,0:T(8,128)S(1)} %get-tuple-element.6), channel_id=2, replica_groups=mesh['turn'=8,'river'=16,'bucket'=4] {'river'}, dimensions={0}, use_global_device_ids=true | all-gather | bytes 721344 | tf_op jit(solution)/shard_map/means/all_gather | solution.py:253
  98.4 0.6 broadcast_multiply_fusion.1
  99.1 20.5 %all-gather.1 = f32[64,1326]{1,0:T(8,128)S(1)} all-gather(f32[8,1326]{1,0:T(8,128)S(1)} %get-tuple-element.7), channel_id=3, replica_groups=mesh['turn'=8,'river'=16,'bucket'=4] {'turn'}, dimensions={0}, use_global_device_ids=true | all-gather | bytes 381888 | tf_op jit(solution)/shard_map/means/all_gather | solution.py:255
  119.6 0.6 broadcast_multiply_fusion
  (4 shorter events, 0.1 us)
Async XLA Ops:
  0.6 0.9 copy-start
  0.6 59.1 %copy-start.4 = (s32[1,2,1326]{2,1,0:T(2,128)S(1)}, s32[1,2,1326]{2,1,0:T(2,128)}, u32[]{:S(2)}) copy-start(s32[1,2,1326]{2,1,0:T(2,128)} %param.12) | copy-start | bytes 31828
  0.7 59.1 %copy-start.3 = (s32[1,2,1326]{2,1,0:T(2,128)S(1)}, s32[1,2,1326]{2,1,0:T(2,128)}, u32[]{:S(2)}) copy-start(s32[1,2,1326]{2,1,0:T(2,128)} %param.10) | copy-start | bytes 31828
  0.7 59.1 %copy-start.2 = (f32[1,2,1326]{2,1,0:T(2,128)S(1)}, f32[1,2,1326]{2,1,0:T(2,128)}, u32[]{:S(2)}) copy-start(f32[1,2,1326]{2,1,0:T(2,128)} %param.9) | copy-start | bytes 31828
  2.3 10.3 %all-to-all-start = ((bf16[4,72,384]{2,1,0:T(8,128)(2,1)}), bf16[4,72,384]{2,1,0:T(8,128)(2,1)S(1)}, u32[]{:S(2)}, u32[]{:S(2)}) async-start(bf16[4,72,384]{2,1,0:T(8,128)(2,1)} %broadcast_in_dim.2), calls=%async_computation | async-start | bytes 442368 | tf_op jit(solution)/shard_map/share_rows/all_to_all | solution.py:198
  12.6 0.7 copy-start.5
  13.2 0.7 copy-start.6
  47.7 12.0 %collective-permute-start = (f32[1152,128]{1,0:T(8,128)S(1)}, f32[1152,128]{1,0:T(8,128)S(1)}, u32[]{:S(2)}, u32[]{:S(2)}) collective-permute-start(f32[1152,128]{1,0:T(8,128)S(1)} %all_gather.13.mine_ref), channel_id=1, source_target_pairs={{0,64},{64,0},{128,192},{192,128},{256,320},{320,256},{384,448},{4... | collective-permute-start | bytes 1769480 | tf_op jit(solution)/shard_map/share_sums/ppermute | solution.py:216
  59.8 2.1 %copy-start.1 = (bf16[1408,1408]{1,0:T(8,128)(2,1)S(1)}, bf16[1408,1408]{1,0:T(8,128)(2,1)}, u32[]{:S(2)}) copy-start(bf16[1408,1408]{1,0:T(8,128)(2,1)} %constant.35.clone.table_ref) | copy-start | bytes 11894788

commit v2 on v1

v2 whole, which is shorter than its diff:
```python
import functools

import jax
import jax.numpy as jnp
import numpy as np
from jax import lax
from jax.experimental import pallas as pl
from jax.experimental.pallas import tpu as pltpu
from jax.sharding import PartitionSpec as P

OPTIONS = 2
REPLIES = 8
LANES = 128
CARDS = 52
CORES = 2
F32 = jnp.float32
BF16 = jnp.bfloat16
I16 = jnp.int16
POT_MOST = 24.0
POT_LEAST = 2.0
CHANCE_LEAST = 0.049804688
CODE_MOST = 32000.0
GATHER_STEP = 512


def card_table(count, padded):
    table = np.zeros((LANES, padded), np.float32)
    for cards in np.triu_indices(CARDS, 1):
        table[cards[:count], np.arange(count)] = 1.0
    return jnp.asarray(table, BF16)


def code_scale(floor, most):
    return CODE_MOST / np.log2(1.0 + most / floor)


def sum_code(hands, depth):
    most = REPLIES * POT_MOST / hands
    floor = POT_LEAST / hands * CHANCE_LEAST**depth
    return floor, code_scale(floor, most)


def encode(x, floor, scale):
    size = jnp.log(1.0 + jnp.abs(x) * (1.0 / floor)) * (scale / np.log(2.0))
    size = jnp.minimum(jnp.floor(size + 0.5), 32767.0)
    return jnp.where(x < 0, -size, size).astype(jnp.int32).astype(I16)


def decode(code, floor, scale):
    code = code.astype(jnp.int32).astype(F32)
    size = (jnp.exp(jnp.abs(code) * (np.log(2.0) / scale)) - 1.0) * floor
    return jnp.where(code < 0, -size, size)


def encode_rows(x, hands):
    most = jnp.maximum(jnp.max(jnp.abs(x), axis=1, keepdims=True), 1e-30)
    power = jnp.floor(jnp.log(most) * (1.0 / np.log(2.0)) + 1.0)
    code = jnp.floor(x * (jnp.exp(power * -np.log(2.0)) * CODE_MOST) + 0.5)
    lane = lax.broadcasted_iota(jnp.int32, x.shape, 1)
    return jnp.where(lane == hands, power, code).astype(jnp.int32).astype(I16)


def decode_rows(code, hands):
    code = code.astype(jnp.int32).astype(F32)
    step = jnp.exp(code[:, hands : hands + 1] * np.log(2.0)) * (1.0 / CODE_MOST)
    return code[:, 0:hands] * step


def split_two(x):
    high = x.astype(BF16)
    return high, (x - high.astype(F32)).astype(BF16)


def split_three(x):
    high = x.astype(BF16)
    rest = x - high.astype(F32)
    middle = rest.astype(BF16)
    return high, middle, (rest - middle.astype(F32)).astype(BF16)


def dot_rows(a, b):
    return lax.dot_general(a, b, (((1,), (1,)), ((), ())), preferred_element_type=F32)


def line_sum_kernel(hand_count, code, rows_ref, acts_ref, info_ref, sums_ref):
    blocks, rows, width = rows_ref.shape
    lines, depth = acts_ref.shape
    entries = lines // (OPTIONS * REPLIES)
    table = rows_ref[...].reshape(blocks * rows, width)
    column = lax.broadcasted_iota(jnp.int32, (lines, width), 1)
    ones = jnp.ones((8, width), BF16)
    product = None
    for step in range(depth):
        picks = (acts_ref[:, step : step + 1] == column).astype(F32).astype(BF16)
        looked = dot_rows(table, picks) + (1.0 - dot_rows(ones, picks)[0:1])
        product = looked if product is None else product * looked
    kind = info_ref[0:1, :]
    scale = info_ref[1:2, :] / hand_count
    sign = jnp.where(kind == 1.0, 1.0, jnp.where(kind == 2.0, -1.0, 0.0))
    weights = (jnp.where(kind == 0.0, scale, 0.0), sign * scale)
    line = lax.broadcasted_iota(jnp.int32, (lines, LANES), 0)
    lane = lax.broadcasted_iota(jnp.int32, (lines, LANES), 1)
    slot = ((line // REPLIES) % OPTIONS) * entries + line // (REPLIES * OPTIONS)
    group = OPTIONS * entries
    total = jnp.zeros((rows, LANES), F32)
    for kind_index, weight in enumerate(weights):
        pieces = split_three(product * weight)
        for block in range(blocks):
            target = slot + (block * 2 + kind_index) * group
            gather = (lane == target).astype(F32).astype(BF16)
            for piece in pieces:
                total += jnp.dot(
                    piece[block * rows : (block + 1) * rows],
                    gather,
                    preferred_element_type=F32,
                )
    codes = encode(total, *code)
    for copy in range(sums_ref.shape[0]):
        sums_ref[copy] = codes


def prepare_kernel(
    shard_rows, half_rows, blocks, held, core_ref, reach_ref, live_ref, rank_ref, bucket_ref,
    cards_ref, contest_ref, rows_ref, turned_ref,
):
    boards, hands = reach_ref.shape
    padded = cards_ref.shape[1]
    core = core_ref[0, 0].astype(F32)
    bucket = bucket_ref[...].astype(F32)
    owner = jnp.floor((bucket + 0.5) * (1.0 / shard_rows))
    row = bucket - owner * shard_rows
    place = jnp.floor((owner + 0.5) * (1.0 / blocks))
    half = jnp.where(row >= half_rows, 1.0, 0.0)
    row = row - half * (shard_rows - half_rows)
    elsewhere = jnp.where(half == core, 0.0, 1.0)
    rows_ref[...] = jnp.full(rows_ref.shape, -1.0, F32)
    rows_ref[0:boards, 0:hands] = elsewhere * held + place * half_rows + row
    rows_ref[boards : 2 * boards, 0:hands] = owner - place * blocks
    rows_ref[2 * boards : 3 * boards, :] = jnp.zeros((boards, rows_ref.shape[1]), F32)
    rows_ref[2 * boards : 3 * boards, 0:hands] = reach_ref[...] * live_ref[...].astype(F32)

    turned_ref[...] = jnp.zeros(turned_ref.shape, F32)
    turned_ref[0:boards, 0:hands] = rank_ref[...].astype(F32)
    rank_rows = turned_ref[0:8, :]
    for start in range(0, padded, LANES):
        ranks = turned_ref[:, start : start + LANES].T
        cards = cards_ref[:, start : start + LANES].astype(F32).T.astype(BF16)
        shared = jnp.dot(cards, cards_ref[...], preferred_element_type=F32)
        for board in range(boards):
            order = rank_rows[board : board + 1, :] - ranks[:, board : board + 1]
            contest = jnp.where(shared == 0.0, jnp.clip(order, -1.0, 1.0), 0.0)
            contest_ref[board, start : start + LANES, :] = contest.astype(BF16)


def board_kernel(
    blocks, in_code, mine_ref, other_ref, live_ref, rows_hbm, cards_hbm, contest_hbm, river_ref,
    part_ref, rows_ref, cards_ref, contest_ref, plain_ref, sums_ref, show_ref, fold_ref,
    total_ref, rows_sem, cards_sem, contest_sem,
):
    rows_copy = pltpu.make_async_copy(rows_hbm, rows_ref, rows_sem)
    cards_copy = pltpu.make_async_copy(cards_hbm, cards_ref, cards_sem)
    contest_copy = pltpu.make_async_copy(contest_hbm, contest_ref, contest_sem)
    rows_copy.start()
    cards_copy.start()
    contest_copy.start()
    boards, hands = live_ref.shape
    padded = cards_ref.shape[1]
    wide = rows_ref.shape[1]
    rivers, half_rows, _ = mine_ref.shape
    held = rivers * half_rows
    slots = 2 * held

    for part, ref in enumerate((mine_ref, other_ref)):
        for river in range(rivers):
            at = part * held + river * half_rows
            plain_ref[at : at + half_rows, :] = decode(ref[river], *in_code)
    for start in range(0, slots, LANES):
        high, low = split_two(plain_ref[start : start + LANES, :].T)
        sums_ref[0:LANES, start : start + LANES] = high
        sums_ref[LANES : 2 * LANES, start : start + LANES] = low

    rows_copy.wait()
    step = GATHER_STEP
    columns = LANES // blocks
    half_columns = columns // 2

    for board in range(boards):

        def gather(turn, carry, board=board):
            lanes = pl.ds(pl.multiple_of(turn * step, step), step)
            index = rows_ref[board : board + 1, lanes].astype(jnp.int32)
            group = rows_ref[boards + board : boards + board + 1, lanes]
            reach = rows_ref[2 * boards + board : 2 * boards + board + 1, lanes]
            position = lax.broadcasted_iota(jnp.int32, (slots, step), 0)
            marks = (position == index).astype(F32).astype(BF16)
            found = jnp.dot(sums_ref[...], marks, preferred_element_type=F32)
            found = found[0:LANES] + found[LANES : 2 * LANES]
            chosen = jnp.zeros((columns, step), F32)
            for which in range(blocks):
                chosen += jnp.where(
                    group == which, found[which * columns : (which + 1) * columns], 0.0
                )
            high, low = split_two(chosen * reach)
            show_ref[board, 0:half_columns, lanes] = high[0:half_columns]
            show_ref[board, half_columns:columns, lanes] = low[0:half_columns]
            base = board * columns
            fold_ref[base : base + half_columns, lanes] = high[half_columns:columns]
            fold_ref[base + half_columns : base + columns, lanes] = low[half_columns:columns]
            return carry

        lax.fori_loop(0, wide // step, gather, 0)

    cards_copy.wait()
    row = lax.broadcasted_iota(jnp.int32, cards_ref.shape, 0)
    cards = jnp.where(row == CARDS, 1.0, cards_ref[...].astype(F32)).astype(BF16)
    folds = fold_ref[:, 0:padded]
    held_by = dot_rows(folds, cards)
    lane = lax.broadcasted_iota(jnp.int32, held_by.shape, 1)
    held_by = jnp.where(lane == CARDS, held_by, -held_by)
    folded = folds.astype(F32)
    for piece in split_three(held_by):
        folded += jnp.dot(piece, cards, preferred_element_type=F32)
    contest_copy.wait()
    total = None
    for board in range(boards):
        shown = jnp.dot(
            show_ref[board, :, 0:padded], contest_ref[board], preferred_element_type=F32
        )
        base = board * columns
        value = shown[0:half_columns] + shown[half_columns:columns]
        value = value + (
            folded[base : base + half_columns] + folded[base + half_columns : base + columns]
        )
        entries = half_columns // OPTIONS
        best = jnp.maximum(value[0:entries], value[entries:half_columns])
        best = best[:, 0:hands] * live_ref[board : board + 1, :].astype(F32)
        river_ref[board] = best
        total = best if total is None else total + best
    total_ref[...] = jnp.zeros(total_ref.shape, F32)
    total_ref[:, 0:hands] = total
    codes = encode_rows(total_ref[...], hands)
    for copy in range(part_ref.shape[0]):
        part_ref[copy] = codes


def river_mean_kernel(share, codes_ref, mean_ref, part_ref, total_ref):
    hands = mean_ref.shape[1]
    total = decode_rows(codes_ref[0], hands)
    for river in range(1, codes_ref.shape[0]):
        total += decode_rows(codes_ref[river], hands)
    mean = total * share
    mean_ref[...] = mean
    total_ref[...] = jnp.zeros(total_ref.shape, F32)
    total_ref[:, 0:hands] = mean
    codes = encode_rows(total_ref[...], hands)
    for copy in range(part_ref.shape[0]):
        part_ref[copy] = codes


def turn_mean_kernel(share, codes_ref, mean_ref):
    hands = mean_ref.shape[1]
    total = decode_rows(codes_ref[0], hands)
    for turn in range(1, codes_ref.shape[0]):
        total += decode_rows(codes_ref[turn], hands)
    mean_ref[...] = total * share


def whole_vmem():
    return pl.BlockSpec(memory_space=pltpu.VMEM)


def local(reach_in, hand_live, hand_rank, hand_bucket, strategy, line_acts, line_kind, line_pot):
    turns_here, rivers_here, hands = reach_in.shape
    boards = turns_here * rivers_here
    shard_rows, width = strategy.shape
    lines = line_acts.shape[0]
    entries = lines // (OPTIONS * REPLIES)
    blocks = lax.axis_size("bucket")
    rivers = lax.axis_size("river")
    turns = lax.axis_size("turn")
    padded = -(-hands // LANES) * LANES
    wide = -(-hands // GATHER_STEP) * GATHER_STEP
    half_rows = -(-shard_rows // (CORES * 8)) * 8
    core = lax.axis_index("turn") % CORES

    with jax.named_scope("share_rows"):
        part = lax.dynamic_slice_in_dim(
            strategy, core * (shard_rows - half_rows), half_rows, axis=0
        )
        rows = lax.all_to_all(
            jnp.broadcast_to(part[None], (blocks, half_rows, width)),
            "bucket",
            split_axis=0,
            concat_axis=0,
            tiled=True,
        )
    in_code = sum_code(hands, line_acts.shape[1])
    info = jnp.stack([line_kind.astype(F32), line_pot])
    with jax.named_scope("line_sums"):
        sums = pl.pallas_call(
            functools.partial(line_sum_kernel, hands, in_code),
            out_shape=jax.ShapeDtypeStruct((rivers, half_rows, LANES), I16),
            in_specs=[whole_vmem()] * 3,
            out_specs=whole_vmem(),
            compiler_params=pltpu.CompilerParams(vmem_limit_bytes=16 * 2**20),
        )(rows, line_acts, info)
    cards = card_table(hands, padded)
    live = hand_live.reshape(boards, hands)
    with jax.named_scope("share_sums"):
        mine = lax.all_to_all(sums, "river", split_axis=0, concat_axis=0, tiled=True)
    with jax.named_scope("prepare"):
        contest, hand_rows = pl.pallas_call(
            functools.partial(prepare_kernel, shard_rows, half_rows, blocks, rivers * half_rows),
            out_shape=(
                jax.ShapeDtypeStruct((boards, padded, padded), BF16),
                jax.ShapeDtypeStruct((8, wide), F32),
            ),
            in_specs=[pl.BlockSpec(memory_space=pltpu.SMEM)] + [whole_vmem()] * 5,
            out_specs=(whole_vmem(), whole_vmem()),
            scratch_shapes=[pltpu.VMEM((LANES, padded), F32)],
            cost_estimate=pl.CostEstimate(
                flops=8 * boards * padded * padded,
                bytes_accessed=(boards + 1) * 2 * padded * padded,
                transcendentals=0,
            ),
            compiler_params=pltpu.CompilerParams(vmem_limit_bytes=24 * 2**20),
        )(
            core.astype(jnp.int32).reshape(1, 1),
            reach_in.reshape(boards, hands),
            live,
            hand_rank.reshape(boards, hands),
            hand_bucket.reshape(boards, hands),
            cards,
        )
    mine, hand_rows = lax.optimization_barrier((mine, hand_rows))
    with jax.named_scope("share_sums"):
        swap = [(device, device ^ 1) for device in range(turns)]
        other = lax.ppermute(mine, "turn", swap)
    with jax.named_scope("boards"):
        slots = 2 * rivers * half_rows
        river, partial = pl.pallas_call(
            functools.partial(board_kernel, blocks, in_code),
            out_shape=(
                jax.ShapeDtypeStruct((boards, entries, hands), F32),
                jax.ShapeDtypeStruct((rivers, entries, padded), I16),
            ),
            in_specs=[whole_vmem()] * 3 + [pl.BlockSpec(memory_space=pltpu.HBM)] * 3,
            out_specs=(whole_vmem(), whole_vmem()),
            scratch_shapes=[
                pltpu.VMEM(hand_rows.shape, F32),
                pltpu.VMEM(cards.shape, BF16),
                pltpu.VMEM(contest.shape, BF16),
                pltpu.VMEM((slots, LANES), F32),
                pltpu.VMEM((2 * LANES, slots), BF16),
                pltpu.VMEM((boards, LANES // blocks, wide), BF16),
                pltpu.VMEM((boards * LANES // blocks, wide), BF16),
                pltpu.VMEM((entries, padded), F32),
                pltpu.SemaphoreType.DMA(()),
                pltpu.SemaphoreType.DMA(()),
                pltpu.SemaphoreType.DMA(()),
            ],
            compiler_params=pltpu.CompilerParams(vmem_limit_bytes=60 * 2**20),
        )(mine, other, live, hand_rows, cards, contest)
    river_value = river.reshape(turns_here, rivers_here, entries, hands)
    with jax.named_scope("means"):
        by_river = lax.all_to_all(partial, "river", split_axis=0, concat_axis=0, tiled=True)
        turn_value, partial = pl.pallas_call(
            functools.partial(river_mean_kernel, 1.0 / (rivers * rivers_here)),
            out_shape=(
                jax.ShapeDtypeStruct((entries, hands), F32),
                jax.ShapeDtypeStruct((turns, entries, padded), I16),
            ),
            in_specs=[whole_vmem()],
            out_specs=(whole_vmem(), whole_vmem()),
            scratch_shapes=[pltpu.VMEM((entries, padded), F32)],
        )(by_river)
        by_turn = lax.all_to_all(partial, "turn", split_axis=0, concat_axis=0, tiled=True)
        flop_value = pl.pallas_call(
            functools.partial(turn_mean_kernel, 1.0 / (turns * turns_here)),
            out_shape=jax.ShapeDtypeStruct((entries, hands), F32),
            in_specs=[whole_vmem()],
            out_specs=whole_vmem(),
        )(by_turn)
    return river_value, turn_value[None], flop_value


def solution(mesh):
    return jax.shard_map(
        local,
        mesh=mesh,
        in_specs=(
            P("turn", "river", None),
            P("turn", "river", None),
            P("turn", "river", None),
            P("turn", "river", None),
            P(("river", "bucket"), None),
            P("bucket", None),
            P("bucket"),
            P("bucket"),
        ),
        out_specs=(
            P("turn", "river", "bucket", None),
            P("turn", "bucket", None),
            P("bucket", None),
        ),
        check_vma=False,
    )
```

time: 121 us -> 108 us (0.89)
  blocking collectives: 76.2 us -> 39.4 us
  starting transfers between devices: 15.4 us -> 29.4 us
  Pallas kernels: 14.6 us -> 18.4 us
  local copies, waits for them, and re-layouts: 7.05 us -> 10.6 us
  waiting for transfers between devices: 4.78 us -> 7.05 us
    all_gather x3 -> x0, blocking collectives: 76.2 us -> none  [the longest x1 32.4 us: local(): mine = lax.all_gather(sums, 'river', axis=0, tiled=True)]
    all_to_all x0 -> x2, blocking collectives: none -> 39.4 us  [the longest x1 21.7 us: local(): lax.all_to_all(partial, 'river', split_axis=0, concat_axis=0, tiled=True)]
    all_to_all x0 -> x1, starting transfers between devices: none -> 14.9 us  [local(): lax.all_to_all(sums, 'river', split_axis=0, concat_axis=0, tiled=True)]
    unnamed x16 -> x21, local copies, waits for them, and re-layouts: 6.04 us -> 9.87 us
    pallas_call x2 -> x5, Pallas kernels: 14.6 us -> 18.4 us  [the longest x1 9.73 us: local(): pl.pallas_call(functools.partial(board_kernel, blocks, in_code), out_shap...]
    all_to_all x0 -> x1, waiting for transfers between devices: none -> 2.66 us  [local(): lax.all_to_all(sums, 'river', split_axis=0, concat_axis=0, tiled=True)]
    all_to_all x1, waiting for transfers between devices: 4.52 us -> 3.2 us  [local(): lax.all_to_all(jnp.broadcast_to(part[None], (blocks, half_rows, width)),...]
    another operation x0 -> x2, other arithmetic: none -> 1.32 us  [local(): info = jnp.stack([line_kind.astype(F32), line_pot])]
  transfers between devices with their start and end apart: 2 -> 3, of which waited for: 2 -> 3; matrix products, arithmetic and copies ran while one was open for 2% -> 2% of each run, Pallas kernels for 0% -> 3%
where the time goes in v2:
time: 108 us; the launch traced here: 107 us
  blocking collectives  39.4 us (36%)
  starting transfers between devices  29.4 us (27%)
  Pallas kernels  18.4 us (17%)
  local copies, waits for them, and re-layouts  10.6 us (10%)
  waiting for transfers between devices  7.05 us (7%)
  other arithmetic  1.32 us (1%)
    all_to_all x1, blocking collectives, local(): lax.all_to_all(partial, 'river', split_axis=0, concat_axis=0, tiled=True)  21.7 us
    all_to_all x1, blocking collectives, local(): lax.all_to_all(partial, 'turn', split_axis=0, concat_axis=0, tiled=True)  17.7 us
    all_to_all x1, starting transfers between devices, local(): lax.all_to_all(sums, 'river', split_axis=0, concat_axis=0, tiled=True)  14.9 us
    unnamed x21, local copies, waits for them, and re-layouts  9.87 us
    pallas_call x1, Pallas kernels, local(): pl.pallas_call(functools.partial(board_kernel, blocks, in_code), out_shap...  9.73 us
    ppermute x1, starting transfers between devices, local(): other = lax.ppermute(mine, 'turn', swap)  9.51 us
    all_to_all x1, starting transfers between devices, local(): lax.all_to_all(jnp.broadcast_to(part[None], (blocks, half_rows, width)),...  5.01 us
    all_to_all x1, waiting for transfers between devices, local(): lax.all_to_all(jnp.broadcast_to(part[None], (blocks, half_rows, width)),...  3.2 us
  transfers between devices with their start and end apart: 3, of which 3 were waited for; matrix products, arithmetic and copies ran while one was open for 2% of the time, Pallas kernels for 3%

profile of v2, /device:TPU:1, one launch (start us, length us, event | category | flops | bytes accessed | tf_op | source)
XLA Modules:
  0.0 107.0 jit_solution(10087065910642173300)
XLA Ops:
  0.6 0.0 copy-start
  0.7 0.9 copy-done
  1.6 0.7 broadcast_in_dim.4
  2.3 5.0 %all-to-all-start = ((bf16[4,72,384]{2,1,0:T(8,128)(2,1)}), bf16[4,72,384]{2,1,0:T(8,128)(2,1)S(1)}, u32[]{:S(2)}, u32[]{:S(2)}) async-start(bf16[4,72,384]{2,1,0:T(8,128)(2,1)} %broadcast_in_dim.4), calls=%async_computation | async-start | bytes 442368 | tf_op jit(solution)/shard_map/share_rows/all_to_all | solution.py:290
  7.3 0.7 convert_bitcast_fusion
  7.9 0.8 copy.12.acts_ref
  8.7 0.7 pad_maximum_fusion.info_ref
  9.4 3.2 %all-to-all-done.rows_ref = bf16[4,72,384]{2,1,0:T(8,128)(2,1)S(1)} async-done(((bf16[4,72,384]{2,1,0:T(8,128)(2,1)}), bf16[4,72,384]{2,1,0:T(8,128)(2,1)S(1)}, u32[]{:S(2)}, u32[]{:S(2)}) %all-to-all-start) | async-done | bytes 221216 | tf_op jit(solution)/shard_map/share_rows/all_to_all | solution.py:290
  12.6 2.2 %line_sums.1 = s16[16,72,128]{2,1,0:T(8,128)(2,1)} custom-call(bf16[4,72,384]{2,1,0:T(8,128)(2,1)S(1)} %all-to-all-done.rows_ref, s32[128,4]{1,0:T(8,128)S(1)} %copy.12.acts_ref, f32[2,128]{1,0:T(2,128)S(1)} %pad_maximum_fusion.info_ref), custom_call_target="tpu_custom_call" | custom-call | tf_op jit(solution)/shard_map/line_sums/pallas_call | solution.py:300
  14.8 14.9 %all-to-all-start.1 = ((s16[16,72,128]{2,1,0:T(8,128)(2,1)}), s16[16,72,128]{2,1,0:T(8,128)(2,1)S(1)}, u32[]{:S(2)}, u32[]{:S(2)}) async-start(s16[16,72,128]{2,1,0:T(8,128)(2,1)} %line_sums.1), calls=%async_computation.1 | async-start | bytes 589824 | tf_op jit(solution)/shard_map/share_sums/all_to_all | solution.py:310
  29.7 0.0 copy-start.2
  29.8 1.0 copy-done.2
  30.7 0.0 copy-start.4
  30.7 0.7 copy-done.4
  31.4 0.0 copy-start.5
  31.4 0.7 copy-done.5
  32.1 0.0 copy-start.6
  32.1 0.7 copy-done.6
  32.8 0.0 copy-start.7
  32.8 0.7 copy-done.7
  33.5 2.9 %prepare.1 = (bf16[2,1408,1408]{2,1,0:T(8,128)(2,1)S(1)}, f32[8,1536]{1,0:T(8,128)S(1)}) custom-call(s32[1,1]{1,0:T(1,128)} %bitcast.2.core_ref, f32[2,1326]{1,0:T(2,128)S(1)} %bitcast.12, s32[2,1326]{1,0:T(2,128)S(1)} %bitcast.11, s32[2,1326]{1,0:T(2,128)S(1)} %bitcast.13, s32[2,1326]{1,0:T(2,128)S(1)} %bitcast.14, bf16[128,1408]{1,0:T(8,128)(2,1)S(1)} %copy-done.2), custom_call_target="tpu_custom_call" | custom-call | flops 31719424 | bytes 11894784 | tf_op jit(solution)/shard_map/prepare/pallas_call | solution.py:312
  36.5 0.0 copy-start.1
  36.5 3.1 %copy-done.1 = bf16[2,1408,1408]{2,1,0:T(8,128)(2,1)} copy-done((bf16[2,1408,1408]{2,1,0:T(8,128)(2,1)}, bf16[2,1408,1408]{2,1,0:T(8,128)(2,1)S(1)}, u32[]{:S(2)}) %copy-start.1) | copy-done | bytes 7929880
  39.6 0.0 copy-start.3
  39.6 0.6 copy-done.3
  40.2 2.7 %all-to-all-done.1.mine_ref = s16[16,72,128]{2,1,0:T(8,128)(2,1)S(1)} async-done(((s16[16,72,128]{2,1,0:T(8,128)(2,1)}), s16[16,72,128]{2,1,0:T(8,128)(2,1)S(1)}, u32[]{:S(2)}, u32[]{:S(2)}) %all-to-all-start.1) | async-done | bytes 294944 | tf_op jit(solution)/shard_map/share_sums/all_to_all | solution.py:310
  42.8 0.0 copy-start.8
  42.8 9.5 %collective-permute-start = (s16[16,72,128]{2,1,0:T(8,128)(2,1)S(1)}, s16[16,72,128]{2,1,0:T(8,128)(2,1)S(1)}, u32[]{:S(2)}, u32[]{:S(2)}) collective-permute-start(s16[16,72,128]{2,1,0:T(8,128)(2,1)S(1)} %all-to-all-done.1.mine_ref), channel_id=1, source_target_pairs={{0,64},{64,0},{128,192},{192,128},{256,320},{320,256},{384,448},{4... | collective-permute-start | bytes 884744 | tf_op jit(solution)/shard_map/share_sums/ppermute | solution.py:338
  52.4 1.2 %collective-permute-done.other_ref = s16[16,72,128]{2,1,0:T(8,128)(2,1)S(1)} collective-permute-done((s16[16,72,128]{2,1,0:T(8,128)(2,1)S(1)}, s16[16,72,128]{2,1,0:T(8,128)(2,1)S(1)}, u32[]{:S(2)}, u32[]{:S(2)}) %collective-permute-start) | collective-permute-done | bytes 294944 | tf_op jit(solution)/shard_map/share_sums/ppermute | solution.py:338
  53.5 0.0 copy-start.9
  53.5 0.0 copy-done.8
  53.6 0.7 copy-done.9
  54.3 9.7 %boards.1 = (f32[2,8,1326]{2,1,0:T(8,128)}, s16[16,8,1408]{2,1,0:T(8,128)(2,1)}) custom-call(s16[16,72,128]{2,1,0:T(8,128)(2,1)} %copy-done.8, s16[16,72,128]{2,1,0:T(8,128)(2,1)} %copy-done.9, s32[2,1326]{1,0:T(2,128)} %bitcast.10, f32[8,1536]{1,0:T(8,128)} %copy-done.3, bf16[128,1408]{1,0:T(8,128)(2,1)} %constant.26.clone.cards_ref.cards_hbm, ...), custom_call_target="tpu_custom_call" | custom-call | tf_op jit(solution)/shard_map/boards/pallas_call | solution.py:341
  64.0 21.7 %all_to_all.20.codes_ref = s16[16,8,1408]{2,1,0:T(8,128)(2,1)} all-to-all(s16[16,8,1408]{2,1,0:T(8,128)(2,1)} %get-tuple-element.16), channel_id=1, replica_groups=mesh['turn'=8,'river'=16,'bucket'=4] {'river'}, dimensions={0} | all-to-all | bytes 720896 | tf_op jit(solution)/shard_map/means/all_to_all | solution.py:366
  85.7 1.9 %means.2 = (f32[8,1326]{1,0:T(8,128)}, s16[8,8,1408]{2,1,0:T(8,128)(2,1)}) custom-call(s16[16,8,1408]{2,1,0:T(8,128)(2,1)} %all_to_all.20.codes_ref), custom_call_target="tpu_custom_call" | custom-call | tf_op jit(solution)/shard_map/means/pallas_call | solution.py:367
  87.6 17.7 %all_to_all.21.codes_ref = s16[8,8,1408]{2,1,0:T(8,128)(2,1)} all-to-all(s16[8,8,1408]{2,1,0:T(8,128)(2,1)} %get-tuple-element.18), channel_id=1, replica_groups=mesh['turn'=8,'river'=16,'bucket'=4] {'turn'}, dimensions={0} | all-to-all | bytes 360448 | tf_op jit(solution)/shard_map/means/all_to_all | solution.py:377
  105.4 1.6 %means.3 = f32[8,1326]{1,0:T(8,128)} custom-call(s16[8,8,1408]{2,1,0:T(8,128)(2,1)} %all_to_all.21.codes_ref), custom_call_target="tpu_custom_call" | custom-call | tf_op jit(solution)/shard_map/means/pallas_call | solution.py:378
  (1 shorter events, 0.0 us)
Async XLA Ops:
  0.6 0.9 copy-start
  2.3 10.3 %all-to-all-start = ((bf16[4,72,384]{2,1,0:T(8,128)(2,1)}), bf16[4,72,384]{2,1,0:T(8,128)(2,1)S(1)}, u32[]{:S(2)}, u32[]{:S(2)}) async-start(bf16[4,72,384]{2,1,0:T(8,128)(2,1)} %broadcast_in_dim.4), calls=%async_computation | async-start | bytes 442368 | tf_op jit(solution)/shard_map/share_rows/all_to_all | solution.py:290
  14.8 28.0 %all-to-all-start.1 = ((s16[16,72,128]{2,1,0:T(8,128)(2,1)}), s16[16,72,128]{2,1,0:T(8,128)(2,1)S(1)}, u32[]{:S(2)}, u32[]{:S(2)}) async-start(s16[16,72,128]{2,1,0:T(8,128)(2,1)} %line_sums.1), calls=%async_computation.1 | async-start | bytes 589824 | tf_op jit(solution)/shard_map/share_sums/all_to_all | solution.py:310
  29.7 1.0 copy-start.2
  30.7 0.7 copy-start.4
  31.4 0.7 copy-start.5
  32.1 0.7 copy-start.6
  32.8 0.7 copy-start.7
  36.5 3.1 %copy-start.1 = (bf16[2,1408,1408]{2,1,0:T(8,128)(2,1)}, bf16[2,1408,1408]{2,1,0:T(8,128)(2,1)S(1)}, u32[]{:S(2)}) copy-start(bf16[2,1408,1408]{2,1,0:T(8,128)(2,1)S(1)} %get-tuple-element.14.contest_hbm) | copy-start | bytes 23789572
  39.6 0.6 copy-start.3
  42.8 10.7 %copy-start.8 = (s16[16,72,128]{2,1,0:T(8,128)(2,1)}, s16[16,72,128]{2,1,0:T(8,128)(2,1)S(1)}, u32[]{:S(2)}) copy-start(s16[16,72,128]{2,1,0:T(8,128)(2,1)S(1)} %all-to-all-done.1.mine_ref) | copy-start | bytes 884740
  42.8 10.7 %collective-permute-start = (s16[16,72,128]{2,1,0:T(8,128)(2,1)S(1)}, s16[16,72,128]{2,1,0:T(8,128)(2,1)S(1)}, u32[]{:S(2)}, u32[]{:S(2)}) collective-permute-start(s16[16,72,128]{2,1,0:T(8,128)(2,1)S(1)} %all-to-all-done.1.mine_ref), channel_id=1, source_target_pairs={{0,64},{64,0},{128,192},{192,128},{256,320},{320,256},{384,448},{4... | collective-permute-start | bytes 884744 | tf_op jit(solution)/shard_map/share_sums/ppermute | solution.py:338
  53.5 0.7 copy-start.9

commit v3 on v2

v3 whole, which is shorter than its diff:
```python
import functools

import jax
import jax.numpy as jnp
import numpy as np
from jax import lax
from jax.experimental import pallas as pl
from jax.experimental.pallas import tpu as pltpu
from jax.sharding import PartitionSpec as P

OPTIONS = 2
REPLIES = 8
LANES = 128
CARDS = 52
CORES = 2
CONTEST_PLACES = 8
SMALL = 8 * 2**20
F32 = jnp.float32
BF16 = jnp.bfloat16
I16 = jnp.int16
POT_MOST = 24.0
POT_LEAST = 2.0
CHANCE_LEAST = 0.049804688
CODE_MOST = 32000.0


def card_table(count, padded):
    table = np.zeros((LANES, padded), np.float32)
    for cards in np.triu_indices(CARDS, 1):
        table[cards[:count], np.arange(count)] = 1.0
    return jnp.asarray(table, BF16)


def code_scale(floor, most):
    return CODE_MOST / np.log2(1.0 + most / floor)


def sum_code(hands, depth):
    most = REPLIES * POT_MOST / hands
    floor = POT_LEAST / hands * CHANCE_LEAST**depth
    return floor, code_scale(floor, most)


def encode(x, floor, scale):
    size = jnp.log(1.0 + jnp.abs(x) * (1.0 / floor)) * (scale / np.log(2.0))
    size = jnp.minimum(jnp.floor(size + 0.5), 32767.0)
    return jnp.where(x < 0, -size, size).astype(jnp.int32).astype(I16)


def decode(code, floor, scale):
    code = code.astype(jnp.int32).astype(F32)
    size = (jnp.exp(jnp.abs(code) * (np.log(2.0) / scale)) - 1.0) * floor
    return jnp.where(code < 0, -size, size)


def encode_rows(x, hands):
    most = jnp.maximum(jnp.max(jnp.abs(x), axis=1, keepdims=True), 1e-30)
    power = jnp.floor(jnp.log(most) * (1.0 / np.log(2.0)) + 1.0)
    code = jnp.floor(x * (jnp.exp(power * -np.log(2.0)) * CODE_MOST) + 0.5)
    lane = lax.broadcasted_iota(jnp.int32, x.shape, 1)
    return jnp.where(lane == hands, power, code).astype(jnp.int32).astype(I16)


def sum_decoded(codes_ref, hands):
    total = None
    for index in range(codes_ref.shape[0]):
        code = codes_ref[index].astype(jnp.int32).astype(F32)
        step = jnp.exp(code[:, hands : hands + 1] * np.log(2.0)) * (1.0 / CODE_MOST)
        part = code * step
        total = part if total is None else total + part
    return total


def split_two(x):
    high = x.astype(BF16)
    return high, (x - high.astype(F32)).astype(BF16)


def split_three(x):
    high = x.astype(BF16)
    rest = x - high.astype(F32)
    middle = rest.astype(BF16)
    return high, middle, (rest - middle.astype(F32)).astype(BF16)


def dot_rows(a, b):
    return lax.dot_general(a, b, (((1,), (1,)), ((), ())), preferred_element_type=F32)


def line_sum_kernel(hand_count, code, rows_ref, acts_ref, info_ref, sums_ref):
    blocks, rows, width = rows_ref.shape
    lines, depth = acts_ref.shape
    entries = lines // (OPTIONS * REPLIES)
    table = [rows_ref[block].astype(F32) for block in range(blocks)]
    table = jnp.concatenate(table, axis=0).astype(BF16)
    column = lax.broadcasted_iota(jnp.int32, (lines, width), 1)
    ones = jnp.ones((8, width), BF16)
    product = None
    for step in range(depth):
        picks = (acts_ref[:, step : step + 1] == column).astype(F32).astype(BF16)
        looked = dot_rows(table, picks) + (1.0 - dot_rows(ones, picks)[0:1])
        product = looked if product is None else product * looked
    kind = info_ref[0:1, :]
    scale = info_ref[1:2, :] / hand_count
    sign = jnp.where(kind == 1.0, 1.0, jnp.where(kind == 2.0, -1.0, 0.0))
    weights = (jnp.where(kind == 0.0, scale, 0.0), sign * scale)
    line = lax.broadcasted_iota(jnp.int32, (lines, LANES), 0)
    lane = lax.broadcasted_iota(jnp.int32, (lines, LANES), 1)
    slot = ((line // REPLIES) % OPTIONS) * entries + line // (REPLIES * OPTIONS)
    group = OPTIONS * entries
    total = jnp.zeros((rows, LANES), F32)
    for kind_index, weight in enumerate(weights):
        pieces = split_two(product * weight)
        for block in range(blocks):
            target = slot + (block * 2 + kind_index) * group
            gather = (lane == target).astype(F32).astype(BF16)
            for piece in pieces:
                total += jnp.dot(
                    piece[block * rows : (block + 1) * rows],
                    gather,
                    preferred_element_type=F32,
                )
    codes = encode(total, *code)
    for copy in range(sums_ref.shape[0]):
        sums_ref[copy] = codes


def prepare_kernel(
    shard_rows, held_rows, blocks, rivers, core_ref, reach_hbm, live_hbm, rank_hbm, bucket_hbm,
    cards_hbm, contest_hbm, rows_ref, slots_ref, token_ref, cards_ref, reach_ref, live_ref, rank_ref,
    bucket_ref, index_ref, turned_ref, contest_ref, in_sems, sems,
):
    arrays = (reach_hbm, live_hbm, rank_hbm, bucket_hbm, cards_hbm)
    places = (reach_ref, live_ref, rank_ref, bucket_ref, cards_ref)
    copies = []
    for index, (array, place) in enumerate(zip(arrays, places)):
        copies.append(pltpu.make_async_copy(array, place, in_sems.at[index]))
        copies[-1].start()
    boards, hands = reach_ref.shape
    padded = cards_ref.shape[1]
    chunks = padded // LANES
    token_ref[...] = jnp.zeros(token_ref.shape, I16)
    for copy in copies:
        copy.wait()
    bucket = bucket_ref[...].astype(F32)
    owner = jnp.floor((bucket + 0.5) * (1.0 / shard_rows))
    row = bucket - owner * shard_rows
    place = jnp.floor((owner + 0.5) * (1.0 / blocks))
    half = jnp.where(row >= held_rows, 1.0, 0.0)
    row = row - half * (shard_rows - held_rows)
    elsewhere = jnp.where(half == core_ref[0, 0].astype(F32), 0.0, 1.0)
    index_ref[...] = jnp.zeros(index_ref.shape, F32)
    index_ref[:, 0:hands] = (elsewhere * rivers + place) * held_rows + row
    slots_ref[...] = jnp.zeros(slots_ref.shape, jnp.int32)
    for board in range(boards):
        for chunk in range(chunks):
            slot = index_ref[board : board + 1, chunk * LANES : (chunk + 1) * LANES]
            at = board * chunks + chunk
            slots_ref[at : at + 1, :] = slot.astype(jnp.int32)
    rows_ref[...] = jnp.zeros(rows_ref.shape, F32)
    rows_ref[0:boards, 0:hands] = owner - place * blocks
    live = live_ref[...].astype(F32)
    rows_ref[boards : 2 * boards, 0:hands] = reach_ref[...] * live
    rows_ref[2 * boards : 3 * boards, 0:hands] = live

    turned_ref[...] = jnp.zeros(turned_ref.shape, F32)
    turned_ref[0:boards, 0:hands] = rank_ref[...].astype(F32)
    rank_rows = turned_ref[0:8, :]
    copies = []
    for chunk in range(chunks):
        lines = pl.ds(chunk * LANES, LANES)
        ranks = turned_ref[:, lines].T
        cards = cards_ref[:, lines].astype(F32).T.astype(BF16)
        shared = jnp.dot(cards, cards_ref[...], preferred_element_type=F32)
        for board in range(boards):
            order = rank_rows[board : board + 1, :] - ranks[:, board : board + 1]
            contest = jnp.where(shared == 0.0, jnp.clip(order, -1.0, 1.0), 0.0)
            contest_ref[board, lines, :] = contest.astype(BF16)
        copy = pltpu.make_async_copy(
            contest_ref.at[:, lines, :], contest_hbm.at[0:boards, lines, :], sems.at[chunk]
        )
        copy.start()
        copies.append(copy)
    for copy in copies:
        copy.wait()


def board_kernel(
    blocks, in_code, mine_ref, other_ref, rows_ref, cards_ref, contest_hbm, slots_hbm, river_hbm,
    part_ref, contest_ref, slots_ref, plain_ref, found_ref, show_ref, fold_ref, river_ref,
    contest_sems, slots_sem, river_sems,
):
    boards, _, hands = river_ref.shape
    padded = cards_ref.shape[1]
    chunks = padded // LANES
    rivers, held_rows, _ = mine_ref.shape
    columns = LANES // blocks
    half = columns // 2
    entries = half // OPTIONS
    slots_copy = pltpu.make_async_copy(slots_hbm, slots_ref, slots_sem)
    slots_copy.start()
    contest_copies = []
    for board in range(boards):
        contest_copies.append(
            pltpu.make_async_copy(
                contest_hbm.at[board], contest_ref.at[board], contest_sems.at[board]
            )
        )
        contest_copies[board].start()

    for part, ref in enumerate((mine_ref, other_ref)):
        for river in range(rivers):
            at = (part * rivers + river) * held_rows
            plain_ref[at : at + held_rows, :] = decode(ref[river], *in_code)
    slots_copy.wait()

    for board in range(boards):

        def gather(chunk, carry, board=board):
            base = pl.multiple_of(chunk * LANES, LANES)
            for hand in range(LANES):
                slot = slots_ref[board * chunks + chunk, hand]
                found_ref[pl.ds(base + hand, 1), :] = plain_ref[pl.ds(slot, 1), :]
            return carry

        lax.fori_loop(0, chunks, gather, 0)

        for chunk in range(chunks):
            lanes = pl.ds(chunk * LANES, LANES)
            found = found_ref[lanes, :].T
            group = rows_ref[board : board + 1, lanes]
            reach = rows_ref[boards + board : boards + board + 1, lanes]
            chosen = jnp.zeros((columns, LANES), F32)
            for which in range(blocks):
                chosen += jnp.where(
                    group == which, found[which * columns : (which + 1) * columns], 0.0
                )
            high, low = split_two(chosen * reach)
            show_ref[board, 0:half, lanes] = high[0:half]
            show_ref[board, half:columns, lanes] = low[0:half]
            base = board * columns
            fold_ref[base : base + half, lanes] = high[half:columns]
            fold_ref[base + half : base + columns, lanes] = low[half:columns]

    row = lax.broadcasted_iota(jnp.int32, cards_ref.shape, 0)
    cards = jnp.where(row == CARDS, 1.0, cards_ref[...].astype(F32)).astype(BF16)
    folds = fold_ref[...]
    held_by = dot_rows(folds, cards)
    lane = lax.broadcasted_iota(jnp.int32, held_by.shape, 1)
    held_by = jnp.where(lane == CARDS, held_by, -held_by)
    folded = folds.astype(F32)
    for piece in split_three(held_by):
        folded += jnp.dot(piece, cards, preferred_element_type=F32)
    total = None
    river_copies = []
    for board in range(boards):
        contest_copies[board].wait()
        shown = jnp.dot(show_ref[board], contest_ref[board], preferred_element_type=F32)
        base = board * columns
        value = shown[0:half] + shown[half:columns]
        value = value + (folded[base : base + half] + folded[base + half : base + columns])
        best = jnp.maximum(value[0:entries], value[entries:half])
        best = best * rows_ref[2 * boards + board : 2 * boards + board + 1, :]
        river_ref[board] = best[:, 0:hands]
        river_copies.append(
            pltpu.make_async_copy(river_ref.at[board], river_hbm.at[board], river_sems.at[board])
        )
        river_copies[board].start()
        total = best if total is None else total + best
    codes = encode_rows(total, hands)
    for copy in range(part_ref.shape[0]):
        part_ref[copy] = codes
    for copy in river_copies:
        copy.wait()


def river_mean_kernel(share, codes_ref, mean_ref, part_ref):
    hands = mean_ref.shape[1]
    mean = sum_decoded(codes_ref, hands) * share
    mean_ref[...] = mean[:, 0:hands]
    lane = lax.broadcasted_iota(jnp.int32, mean.shape, 1)
    codes = encode_rows(jnp.where(lane < hands, mean, 0.0), hands)
    for copy in range(part_ref.shape[0]):
        part_ref[copy] = codes


def turn_mean_kernel(share, codes_ref, turn_ref, turn_out_ref, mean_ref):
    hands = mean_ref.shape[1]
    turn_out_ref[...] = turn_ref[...]
    mean_ref[...] = sum_decoded(codes_ref, hands)[:, 0:hands] * share


def follow_kernel(value_ref, token_ref, out_ref):
    del value_ref, token_ref, out_ref


def whole_vmem():
    return pl.BlockSpec(memory_space=pltpu.VMEM)


def local(reach_in, hand_live, hand_rank, hand_bucket, strategy, line_acts, line_kind, line_pot):
    turns_here, rivers_here, hands = reach_in.shape
    boards = turns_here * rivers_here
    shard_rows, width = strategy.shape
    lines = line_acts.shape[0]
    entries = lines // (OPTIONS * REPLIES)
    blocks = lax.axis_size("bucket")
    rivers = lax.axis_size("river")
    turns = lax.axis_size("turn")
    padded = -(-hands // LANES) * LANES
    held_rows = -(-shard_rows // (CORES * 8)) * 8
    core = lax.axis_index("turn") % CORES

    with jax.named_scope("share_rows"):
        first = core * (shard_rows - held_rows)
        part = lax.dynamic_slice_in_dim(strategy, first, held_rows, axis=0)
        rows = lax.all_to_all(
            jnp.broadcast_to(part[None], (blocks, held_rows, width)),
            "bucket",
            split_axis=0,
            concat_axis=0,
            tiled=True,
        )
    in_code = sum_code(hands, line_acts.shape[1])
    info = jnp.stack([line_kind.astype(F32), line_pot])
    with jax.named_scope("line_sums"):
        sums = pl.pallas_call(
            functools.partial(line_sum_kernel, hands, in_code),
            out_shape=jax.ShapeDtypeStruct((rivers, held_rows, LANES), I16),
            in_specs=[whole_vmem()] * 3,
            out_specs=whole_vmem(),
            compiler_params=pltpu.CompilerParams(vmem_limit_bytes=16 * 2**20),
        )(rows, line_acts, info)
    cards = card_table(hands, padded)
    live = hand_live.reshape(boards, hands)
    with jax.named_scope("share_sums"):
        mine = lax.all_to_all(sums, "river", split_axis=0, concat_axis=0, tiled=True)
    with jax.named_scope("prepare"):
        chunks = padded // LANES
        slot_shape = (-(-boards * chunks // 8) * 8, LANES)
        contest, hand_rows, slots, token, cards = pl.pallas_call(
            functools.partial(prepare_kernel, shard_rows, held_rows, blocks, rivers),
            out_shape=(
                jax.ShapeDtypeStruct((CONTEST_PLACES, padded, padded), BF16),
                jax.ShapeDtypeStruct((8, padded), F32),
                jax.ShapeDtypeStruct(slot_shape, jnp.int32),
                jax.ShapeDtypeStruct((16, LANES), I16),
                jax.ShapeDtypeStruct(cards.shape, BF16),
            ),
            in_specs=[pl.BlockSpec(memory_space=pltpu.SMEM)]
            + [pl.BlockSpec(memory_space=pl.ANY)] * 5,
            out_specs=(pl.BlockSpec(memory_space=pl.ANY),) + (whole_vmem(),) * 4,
            scratch_shapes=[
                pltpu.VMEM((boards, hands), F32),
                pltpu.VMEM((boards, hands), jnp.int32),
                pltpu.VMEM((boards, hands), jnp.int32),
                pltpu.VMEM((boards, hands), jnp.int32),
                pltpu.VMEM((boards, padded), F32),
                pltpu.VMEM((LANES, padded), F32),
                pltpu.VMEM((boards, padded, padded), BF16),
                pltpu.SemaphoreType.DMA((5,)),
                pltpu.SemaphoreType.DMA((chunks,)),
            ],
            cost_estimate=pl.CostEstimate(
                flops=8 * boards * padded * padded,
                bytes_accessed=(boards + 1) * 2 * padded * padded,
                transcendentals=0,
            ),
            compiler_params=pltpu.CompilerParams(vmem_limit_bytes=40 * 2**20),
        )(
            core.astype(jnp.int32).reshape(1, 1),
            reach_in.reshape(boards, hands),
            live,
            hand_rank.reshape(boards, hands),
            hand_bucket.reshape(boards, hands),
            cards,
        )
    with jax.named_scope("share_sums"):
        mine = pl.pallas_call(
            follow_kernel,
            out_shape=jax.ShapeDtypeStruct(mine.shape, mine.dtype),
            in_specs=[whole_vmem()] * 2,
            out_specs=whole_vmem(),
            input_output_aliases={0: 0},
            compiler_params=pltpu.CompilerParams(vmem_limit_bytes=SMALL),
        )(mine, token)
        swap = [(device, device ^ 1) for device in range(turns)]
        other = lax.ppermute(mine, "turn", swap)
    with jax.named_scope("boards"):
        river, partial = pl.pallas_call(
            functools.partial(board_kernel, blocks, in_code),
            out_shape=(
                jax.ShapeDtypeStruct((boards, entries, hands), F32),
                jax.ShapeDtypeStruct((rivers, entries, padded), I16),
            ),
            in_specs=[whole_vmem()] * 4 + [pl.BlockSpec(memory_space=pl.ANY)] * 2,
            out_specs=(pl.BlockSpec(memory_space=pl.ANY), whole_vmem()),
            scratch_shapes=[
                pltpu.VMEM((boards, padded, padded), BF16),
                pltpu.SMEM(slots.shape, jnp.int32),
                pltpu.VMEM((CORES * rivers * held_rows, LANES), F32),
                pltpu.VMEM((padded, LANES), F32),
                pltpu.VMEM((boards, LANES // blocks, padded), BF16),
                pltpu.VMEM((boards * LANES // blocks, padded), BF16),
                pltpu.VMEM((boards, entries, hands), F32),
                pltpu.SemaphoreType.DMA((boards,)),
                pltpu.SemaphoreType.DMA(()),
                pltpu.SemaphoreType.DMA((boards,)),
            ],
            compiler_params=pltpu.CompilerParams(vmem_limit_bytes=40 * 2**20),
        )(mine, other, hand_rows, cards, contest, slots)
    with jax.named_scope("means"):
        by_river = lax.all_to_all(partial, "river", split_axis=0, concat_axis=0, tiled=True)
        turn_value, partial = pl.pallas_call(
            functools.partial(river_mean_kernel, 1.0 / (rivers * rivers_here)),
            out_shape=(
                jax.ShapeDtypeStruct((entries, hands), F32),
                jax.ShapeDtypeStruct((turns, entries, padded), I16),
            ),
            in_specs=[whole_vmem()],
            out_specs=(whole_vmem(), whole_vmem()),
            compiler_params=pltpu.CompilerParams(vmem_limit_bytes=SMALL),
        )(by_river)
        by_turn = lax.all_to_all(partial, "turn", split_axis=0, concat_axis=0, tiled=True)
        turn_value, flop_value = pl.pallas_call(
            functools.partial(turn_mean_kernel, 1.0 / (turns * turns_here)),
            out_shape=(
                jax.ShapeDtypeStruct(turn_value.shape, F32),
                jax.ShapeDtypeStruct((entries, hands), F32),
            ),
            in_specs=[whole_vmem()] * 2,
            out_specs=(whole_vmem(), whole_vmem()),
            compiler_params=pltpu.CompilerParams(vmem_limit_bytes=SMALL),
        )(by_turn, turn_value)
    river_value = river.reshape(turns_here, rivers_here, entries, hands)
    return river_value, turn_value[None], flop_value


def solution(mesh):
    return jax.shard_map(
        local,
        mesh=mesh,
        in_specs=(
            P("turn", "river", None),
            P("turn", "river", None),
            P("turn", "river", None),
            P("turn", "river", None),
            P(("river", "bucket"), None),
            P("bucket", None),
            P("bucket"),
            P("bucket"),
        ),
        out_specs=(
            P("turn", "river", "bucket", None),
            P("turn", "bucket", None),
            P("bucket", None),
        ),
        check_vma=False,
    )
```

time: 108 us -> 101 us (0.935)
  local copies, waits for them, and re-layouts: 10.6 us -> 6.19 us
  Pallas kernels: 18.4 us -> 15 us
  waiting for transfers between devices: 7.05 us -> 8.62 us
    unnamed x21 -> x13, local copies, waits for them, and re-layouts: 9.87 us -> 5.46 us
    pallas_call x1, Pallas kernels: 9.73 us -> 7.06 us  [local(): pl.pallas_call(functools.partial(board_kernel, blocks, in_code), out_shap...]
    pallas_call x1 -> x2, Pallas kernels: 2.94 us -> 5.05 us  [the longest x1 5.05 us: local(): pl.pallas_call(functools.partial(prepare_kernel, shard_rows, held_rows, b...]
    pallas_call x1, Pallas kernels: 1.89 us -> 0.25 us  [local(): pl.pallas_call(functools.partial(river_mean_kernel, 1.0 / (rivers * river...]
    all_to_all x1, waiting for transfers between devices: 2.66 us -> 4.23 us  [local(): lax.all_to_all(sums, 'river', split_axis=0, concat_axis=0, tiled=True)]
  transfers between devices with their start and end apart: 3 -> 3, of which waited for: 3 -> 3; matrix products, arithmetic and copies ran while one was open for 2% -> 2% of each run, Pallas kernels for 3% -> 5%
where the time goes in v3:
time: 101 us; the launch traced here: 100 us
  blocking collectives  38.8 us (38%)
  starting transfers between devices  29.4 us (29%)
  Pallas kernels  15 us (15%)
  waiting for transfers between devices  8.62 us (9%)
  local copies, waits for them, and re-layouts  6.19 us (6%)
  other arithmetic  1.32 us (1%)
    all_to_all x1, blocking collectives, local(): lax.all_to_all(partial, 'river', split_axis=0, concat_axis=0, tiled=True)  21.4 us
    all_to_all x1, blocking collectives, local(): lax.all_to_all(partial, 'turn', split_axis=0, concat_axis=0, tiled=True)  17.4 us
    all_to_all x1, starting transfers between devices, local(): lax.all_to_all(sums, 'river', split_axis=0, concat_axis=0, tiled=True)  14.9 us
    ppermute x1, starting transfers between devices, local(): other = lax.ppermute(mine, 'turn', swap)  9.51 us
    pallas_call x1, Pallas kernels, local(): pl.pallas_call(functools.partial(board_kernel, blocks, in_code), out_shap...  7.06 us
    unnamed x13, local copies, waits for them, and re-layouts  5.46 us
    pallas_call x1, Pallas kernels, local(): pl.pallas_call(functools.partial(prepare_kernel, shard_rows, held_rows, b...  5.05 us
    all_to_all x1, starting transfers between devices, local(): lax.all_to_all(jnp.broadcast_to(part[None], (blocks, held_rows, width)),...  5.01 us
  transfers between devices with their start and end apart: 3, of which 3 were waited for; matrix products, arithmetic and copies ran while one was open for 2% of the time, Pallas kernels for 5%

profile of v3, /device:TPU:1, one launch (start us, length us, event | category | flops | bytes accessed | tf_op | source)
XLA Modules:
  0.0 100.1 jit_solution(17312511807469582531)
XLA Ops:
  0.6 0.0 copy-start
  0.7 0.9 copy-done
  1.6 0.7 broadcast_in_dim.4
  2.3 5.0 %all-to-all-start = ((bf16[4,72,384]{2,1,0:T(8,128)(2,1)}), bf16[4,72,384]{2,1,0:T(8,128)(2,1)S(1)}, u32[]{:S(2)}, u32[]{:S(2)}) async-start(bf16[4,72,384]{2,1,0:T(8,128)(2,1)} %broadcast_in_dim.4), calls=%async_computation | async-start | bytes 442368 | tf_op jit(solution)/shard_map/share_rows/all_to_all | solution.py:317
  7.3 0.7 convert_bitcast_fusion
  7.9 0.8 copy.13.acts_ref
  8.7 0.7 pad_maximum_fusion.info_ref
  9.4 3.2 %all-to-all-done.rows_ref = bf16[4,72,384]{2,1,0:T(8,128)(2,1)S(1)} async-done(((bf16[4,72,384]{2,1,0:T(8,128)(2,1)}), bf16[4,72,384]{2,1,0:T(8,128)(2,1)S(1)}, u32[]{:S(2)}, u32[]{:S(2)}) %all-to-all-start) | async-done | bytes 221216 | tf_op jit(solution)/shard_map/share_rows/all_to_all | solution.py:317
  12.6 1.9 %line_sums.1 = s16[16,72,128]{2,1,0:T(8,128)(2,1)} custom-call(bf16[4,72,384]{2,1,0:T(8,128)(2,1)S(1)} %all-to-all-done.rows_ref, s32[128,4]{1,0:T(8,128)S(1)} %copy.13.acts_ref, f32[2,128]{1,0:T(2,128)S(1)} %pad_maximum_fusion.info_ref), custom_call_target="tpu_custom_call" | custom-call | tf_op jit(solution)/shard_map/line_sums/pallas_call | solution.py:327
  14.5 14.9 %all-to-all-start.1 = ((s16[16,72,128]{2,1,0:T(8,128)(2,1)}), s16[16,72,128]{2,1,0:T(8,128)(2,1)S(1)}, u32[]{:S(2)}, u32[]{:S(2)}) async-start(s16[16,72,128]{2,1,0:T(8,128)(2,1)} %line_sums.1), calls=%async_computation.1 | async-start | bytes 589824 | tf_op jit(solution)/shard_map/share_sums/all_to_all | solution.py:337
  29.5 0.0 copy-start.1
  29.5 1.0 copy-done.1
  30.4 0.0 copy-start.2
  30.4 0.7 copy-done.2
  31.1 0.0 copy-start.3
  31.1 0.7 copy-done.3
  31.9 0.0 copy-start.4
  31.9 0.7 copy-done.4
  32.6 0.0 copy-start.5
  32.6 0.7 copy-done.5
  33.3 5.0 %prepare.1 = (bf16[8,1408,1408]{2,1,0:T(8,128)(2,1)}, f32[8,1408]{1,0:T(8,128)S(1)}, s32[24,128]{1,0:T(8,128)S(1)}, s16[16,128]{1,0:T(8,128)(2,1)S(1)}, bf16[128,1408]{1,0:T(8,128)(2,1)S(1)}) custom-call(s32[1,1]{1,0:T(1,128)} %bitcast.2.core_ref, f32[2,1326]{1,0:T(2,128)S(1)} %bitcast.10, s32[2,1326]{1,0:T(2,128)S(1)} %bitcast.11, s32[2,1326]{1,0:T(2,128)S(1)} %bitcast.12, ...), custom_call_target="tpu_custom_call" | custom-call | flops 31719424 | bytes 11894784 | tf_op jit(solution)/shard_map/prepare/pallas_call | solution.py:341
  38.3 4.2 %all-to-all-done.1.value_ref = s16[16,72,128]{2,1,0:T(8,128)(2,1)S(1)} async-done(((s16[16,72,128]{2,1,0:T(8,128)(2,1)}), s16[16,72,128]{2,1,0:T(8,128)(2,1)S(1)}, u32[]{:S(2)}, u32[]{:S(2)}) %all-to-all-start.1) | async-done | bytes 294944 | tf_op jit(solution)/shard_map/share_sums/all_to_all | solution.py:337
  42.6 9.5 %collective-permute-start = (s16[16,72,128]{2,1,0:T(8,128)(2,1)S(1)}, s16[16,72,128]{2,1,0:T(8,128)(2,1)S(1)}, u32[]{:S(2)}, u32[]{:S(2)}) collective-permute-start(s16[16,72,128]{2,1,0:T(8,128)(2,1)S(1)} %share_sums.1.mine_ref), channel_id=1, source_target_pairs={{0,64},{64,0},{128,192},{192,128},{256,320},{320,256},{384,448},{4... | collective-permute-start | bytes 884744 | tf_op jit(solution)/shard_map/share_sums/ppermute | solution.py:388
  52.1 1.2 %collective-permute-done.other_ref = s16[16,72,128]{2,1,0:T(8,128)(2,1)S(1)} collective-permute-done((s16[16,72,128]{2,1,0:T(8,128)(2,1)S(1)}, s16[16,72,128]{2,1,0:T(8,128)(2,1)S(1)}, u32[]{:S(2)}, u32[]{:S(2)}) %collective-permute-start) | collective-permute-done | bytes 294944 | tf_op jit(solution)/shard_map/share_sums/ppermute | solution.py:388
  53.3 7.1 %boards.1 = (f32[2,8,1326]{2,1,0:T(8,128)}, s16[16,8,1408]{2,1,0:T(8,128)(2,1)S(1)}) custom-call(s16[16,72,128]{2,1,0:T(8,128)(2,1)S(1)} %share_sums.1.mine_ref, s16[16,72,128]{2,1,0:T(8,128)(2,1)S(1)} %collective-permute-done.other_ref, f32[8,1408]{1,0:T(8,128)S(1)} %get-tuple-element.15.rows_ref, bf16[128,1408]{1,0:T(8,128)(2,1)S(1)} %get-tuple-element.16.cards_ref, ...), custom_call_target="tpu_custom_call" | custom-call | tf_op jit(solution)/shard_map/boards/pallas_call | solution.py:390
  60.3 21.4 %all_to_all.20.codes_ref = s16[16,8,1408]{2,1,0:T(8,128)(2,1)S(1)} all-to-all(s16[16,8,1408]{2,1,0:T(8,128)(2,1)S(1)} %get-tuple-element.20), channel_id=1, replica_groups=mesh['turn'=8,'river'=16,'bucket'=4] {'river'}, dimensions={0} | all-to-all | bytes 720896 | tf_op jit(solution)/shard_map/means/all_to_all | solution.py:413
  81.7 0.3 means.2
  82.0 17.4 %all_to_all.21.codes_ref = s16[8,8,1408]{2,1,0:T(8,128)(2,1)S(1)} all-to-all(s16[8,8,1408]{2,1,0:T(8,128)(2,1)S(1)} %get-tuple-element.21), channel_id=1, replica_groups=mesh['turn'=8,'river'=16,'bucket'=4] {'turn'}, dimensions={0} | all-to-all | bytes 360448 | tf_op jit(solution)/shard_map/means/all_to_all | solution.py:424
  99.4 0.7 means.3
  (2 shorter events, 0.0 us)
Async XLA Ops:
  0.6 0.9 copy-start
  2.3 10.3 %all-to-all-start = ((bf16[4,72,384]{2,1,0:T(8,128)(2,1)}), bf16[4,72,384]{2,1,0:T(8,128)(2,1)S(1)}, u32[]{:S(2)}, u32[]{:S(2)}) async-start(bf16[4,72,384]{2,1,0:T(8,128)(2,1)} %broadcast_in_dim.4), calls=%async_computation | async-start | bytes 442368 | tf_op jit(solution)/shard_map/share_rows/all_to_all | solution.py:317
  14.5 28.0 %all-to-all-start.1 = ((s16[16,72,128]{2,1,0:T(8,128)(2,1)}), s16[16,72,128]{2,1,0:T(8,128)(2,1)S(1)}, u32[]{:S(2)}, u32[]{:S(2)}) async-start(s16[16,72,128]{2,1,0:T(8,128)(2,1)} %line_sums.1), calls=%async_computation.1 | async-start | bytes 589824 | tf_op jit(solution)/shard_map/share_sums/all_to_all | solution.py:337
  29.5 1.0 copy-start.1
  30.4 0.7 copy-start.2
  31.1 0.7 copy-start.3
  31.9 0.7 copy-start.4
  32.6 0.7 copy-start.5
  42.6 10.7 %collective-permute-start = (s16[16,72,128]{2,1,0:T(8,128)(2,1)S(1)}, s16[16,72,128]{2,1,0:T(8,128)(2,1)S(1)}, u32[]{:S(2)}, u32[]{:S(2)}) collective-permute-start(s16[16,72,128]{2,1,0:T(8,128)(2,1)S(1)} %share_sums.1.mine_ref), channel_id=1, source_target_pairs={{0,64},{64,0},{128,192},{192,128},{256,320},{320,256},{384,448},{4... | collective-permute-start | bytes 884744 | tf_op jit(solution)/shard_map/share_sums/ppermute | solution.py:388

commit v4 on v3

--- a/solution.py
+++ b/solution.py
@@ -12,6 +12,7 @@
 REPLIES = 8
 LANES = 128
 CARDS = 52
+TILE = 16
 CORES = 2
 CONTEST_PLACES = 8
 SMALL = 8 * 2**20
@@ -87,46 +88,51 @@
     return lax.dot_general(a, b, (((1,), (1,)), ((), ())), preferred_element_type=F32)
 
 
-def line_sum_kernel(hand_count, code, rows_ref, acts_ref, info_ref, sums_ref):
+def line_sum_kernel(hand_count, code, rows_ref, info_ref, sums_ref):
     blocks, rows, width = rows_ref.shape
-    lines, depth = acts_ref.shape
+    depth, lines = info_ref.shape
+    depth -= 2
     entries = lines // (OPTIONS * REPLIES)
     table = [rows_ref[block].astype(F32) for block in range(blocks)]
     table = jnp.concatenate(table, axis=0).astype(BF16)
-    column = lax.broadcasted_iota(jnp.int32, (lines, width), 1)
-    ones = jnp.ones((8, width), BF16)
-    product = None
-    for step in range(depth):
-        picks = (acts_ref[:, step : step + 1] == column).astype(F32).astype(BF16)
-        looked = dot_rows(table, picks) + (1.0 - dot_rows(ones, picks)[0:1])
-        product = looked if product is None else product * looked
-    kind = info_ref[0:1, :]
-    scale = info_ref[1:2, :] / hand_count
+    column = lax.broadcasted_iota(jnp.int32, (width, lines), 0).astype(F32)
+    picks = [
+        (column == info_ref[step : step + 1, :]).astype(F32).astype(BF16) for step in range(depth)
+    ]
+    picks = jnp.concatenate(picks, axis=1)
+    present = jnp.dot(jnp.ones((8, width), BF16), picks, preferred_element_type=F32)
+    looked = jnp.dot(table, picks, preferred_element_type=F32) + (1.0 - present[0:1])
+    product = looked[:, 0:lines]
+    for step in range(1, depth):
+        product = product * looked[:, step * lines : (step + 1) * lines]
+    kind = info_ref[depth : depth + 1, :]
+    scale = info_ref[depth + 1 : depth + 2, :] / hand_count
     sign = jnp.where(kind == 1.0, 1.0, jnp.where(kind == 2.0, -1.0, 0.0))
     weights = (jnp.where(kind == 0.0, scale, 0.0), sign * scale)
     line = lax.broadcasted_iota(jnp.int32, (lines, LANES), 0)
     lane = lax.broadcasted_iota(jnp.int32, (lines, LANES), 1)
     slot = ((line // REPLIES) % OPTIONS) * entries + line // (REPLIES * OPTIONS)
     group = OPTIONS * entries
-    total = jnp.zeros((rows, LANES), F32)
+    terms, targets = [], []
     for kind_index, weight in enumerate(weights):
-        pieces = split_two(product * weight)
-        for block in range(blocks):
-            target = slot + (block * 2 + kind_index) * group
-            gather = (lane == target).astype(F32).astype(BF16)
-            for piece in pieces:
-                total += jnp.dot(
-                    piece[block * rows : (block + 1) * rows],
-                    gather,
-                    preferred_element_type=F32,
-                )
+        terms.extend(split_three(product * weight))
+        targets.extend([(lane == slot + kind_index * group).astype(F32).astype(BF16)] * 3)
+    summed = jnp.dot(
+        jnp.concatenate(terms, axis=1),
+        jnp.concatenate(targets, axis=0),
+        preferred_element_type=F32,
+    )
+    total = summed[0:rows]
+    for block in range(1, blocks):
+        part = summed[block * rows : (block + 1) * rows]
+        total += pltpu.roll(part, block * 2 * group, 1)
     codes = encode(total, *code)
     for copy in range(sums_ref.shape[0]):
         sums_ref[copy] = codes
 
 
 def prepare_kernel(
-    shard_rows, held_rows, blocks, rivers, core_ref, reach_hbm, live_hbm, rank_hbm, bucket_hbm,
+    shard_rows, held_rows, blocks, rivers, reach_hbm, live_hbm, rank_hbm, bucket_hbm,
     cards_hbm, contest_hbm, rows_ref, slots_ref, token_ref, cards_ref, reach_ref, live_ref, rank_ref,
     bucket_ref, index_ref, turned_ref, contest_ref, in_sems, sems,
 ):
@@ -148,7 +154,8 @@
     place = jnp.floor((owner + 0.5) * (1.0 / blocks))
     half = jnp.where(row >= held_rows, 1.0, 0.0)
     row = row - half * (shard_rows - held_rows)
-    elsewhere = jnp.where(half == core_ref[0, 0].astype(F32), 0.0, 1.0)
+    core = lax.rem(lax.axis_index("turn"), CORES).astype(F32)
+    elsewhere = jnp.where(half == core, 0.0, 1.0)
     index_ref[...] = jnp.zeros(index_ref.shape, F32)
     index_ref[:, 0:hands] = (elsewhere * rivers + place) * held_rows + row
     slots_ref[...] = jnp.zeros(slots_ref.shape, jnp.int32)
@@ -181,6 +188,10 @@
         )
         copy.start()
         copies.append(copy)
+    around = cards_ref[TILE * (CARDS // TILE) : TILE * (CARDS // TILE + 1), :].astype(F32)
+    row = lax.broadcasted_iota(jnp.int32, around.shape, 0)
+    around = jnp.where(row == CARDS % TILE, 1.0, around).astype(BF16)
+    cards_ref[TILE * (CARDS // TILE) : TILE * (CARDS // TILE + 1), :] = around
     for copy in copies:
         copy.wait()
 
@@ -238,27 +249,29 @@
             high, low = split_two(chosen * reach)
             show_ref[board, 0:half, lanes] = high[0:half]
             show_ref[board, half:columns, lanes] = low[0:half]
-            base = board * columns
+            base = board * half
             fold_ref[base : base + half, lanes] = high[half:columns]
-            fold_ref[base + half : base + columns, lanes] = low[half:columns]
-
-    row = lax.broadcasted_iota(jnp.int32, cards_ref.shape, 0)
-    cards = jnp.where(row == CARDS, 1.0, cards_ref[...].astype(F32)).astype(BF16)
+            base = (boards + board) * half
+            fold_ref[base : base + half, lanes] = low[half:columns]
+
+    cards = cards_ref[...]
     folds = fold_ref[...]
     held_by = dot_rows(folds, cards)
+    held_by = held_by[0 : boards * half] + held_by[boards * half : 2 * boards * half]
     lane = lax.broadcasted_iota(jnp.int32, held_by.shape, 1)
     held_by = jnp.where(lane == CARDS, held_by, -held_by)
-    folded = folds.astype(F32)
-    for piece in split_three(held_by):
-        folded += jnp.dot(piece, cards, preferred_element_type=F32)
+    spread = jnp.dot(
+        jnp.concatenate(split_three(held_by), axis=0), cards, preferred_element_type=F32
+    )
+    folded = folds[0 : boards * half].astype(F32) + folds[boards * half :].astype(F32)
+    for piece in range(3):
+        folded += spread[piece * boards * half : (piece + 1) * boards * half]
     total = None
     river_copies = []
     for board in range(boards):
         contest_copies[board].wait()
         shown = jnp.dot(show_ref[board], contest_ref[board], preferred_element_type=F32)
-        base = board * columns
-        value = shown[0:half] + shown[half:columns]
-        value = value + (folded[base : base + half] + folded[base + half : base + columns])
+        value = shown[0:half] + shown[half:columns] + folded[board * half : (board + 1) * half]
         best = jnp.maximum(value[0:entries], value[entries:half])
         best = best * rows_ref[2 * boards + board : 2 * boards + board + 1, :]
         river_ref[board] = best[:, 0:hands]
@@ -322,15 +335,16 @@
             tiled=True,
         )
     in_code = sum_code(hands, line_acts.shape[1])
-    info = jnp.stack([line_kind.astype(F32), line_pot])
+    info = [line_acts.T.astype(F32), line_kind.astype(F32)[None], line_pot[None]]
+    info = jnp.concatenate(info, axis=0)
     with jax.named_scope("line_sums"):
         sums = pl.pallas_call(
             functools.partial(line_sum_kernel, hands, in_code),
             out_shape=jax.ShapeDtypeStruct((rivers, held_rows, LANES), I16),
-            in_specs=[whole_vmem()] * 3,
+            in_specs=[whole_vmem()] * 2,
             out_specs=whole_vmem(),
             compiler_params=pltpu.CompilerParams(vmem_limit_bytes=16 * 2**20),
-        )(rows, line_acts, info)
+        )(rows, info)
     cards = card_table(hands, padded)
     live = hand_live.reshape(boards, hands)
     with jax.named_scope("share_sums"):
@@ -347,8 +361,7 @@
                 jax.ShapeDtypeStruct((16, LANES), I16),
                 jax.ShapeDtypeStruct(cards.shape, BF16),
             ),
-            in_specs=[pl.BlockSpec(memory_space=pltpu.SMEM)]
-            + [pl.BlockSpec(memory_space=pl.ANY)] * 5,
+            in_specs=[pl.BlockSpec(memory_space=pl.ANY)] * 5,
             out_specs=(pl.BlockSpec(memory_space=pl.ANY),) + (whole_vmem(),) * 4,
             scratch_shapes=[
                 pltpu.VMEM((boards, hands), F32),
@@ -368,7 +381,6 @@
             ),
             compiler_params=pltpu.CompilerParams(vmem_limit_bytes=40 * 2**20),
         )(
-            core.astype(jnp.int32).reshape(1, 1),
             reach_in.reshape(boards, hands),
             live,
             hand_rank.reshape(boards, hands),

time: 101 us -> 100 us (0.990)
    another operation x2 -> x0, other arithmetic: 1.32 us -> none  [local(): info = jnp.stack([line_kind.astype(F32), line_pot])]
    unnamed x13 -> x12, local copies, waits for them, and re-layouts: 5.46 us -> 4.68 us
where the time goes in v4:
time: 100 us; the launch traced here: 99.5 us
  blocking collectives  38.8 us (39%)
  starting transfers between devices  29.4 us (29%)
  Pallas kernels  14.3 us (14%)
  waiting for transfers between devices  8.75 us (9%)
  local copies, waits for them, and re-layouts  5.4 us (5%)
  other arithmetic  2 us (2%)
    all_to_all x1, blocking collectives, local(): lax.all_to_all(partial, 'river', split_axis=0, concat_axis=0, tiled=True)  21.4 us
    all_to_all x1, blocking collectives, local(): lax.all_to_all(partial, 'turn', split_axis=0, concat_axis=0, tiled=True)  17.4 us
    all_to_all x1, starting transfers between devices, local(): lax.all_to_all(sums, 'river', split_axis=0, concat_axis=0, tiled=True)  14.9 us
    ppermute x1, starting transfers between devices, local(): other = lax.ppermute(mine, 'turn', swap)  9.52 us
    pallas_call x1, Pallas kernels, local(): pl.pallas_call(functools.partial(board_kernel, blocks, in_code), out_shap...  6.76 us
    pallas_call x1, Pallas kernels, local(): pl.pallas_call(functools.partial(prepare_kernel, shard_rows, held_rows, b...  5.03 us
    all_to_all x1, starting transfers between devices, local(): lax.all_to_all(jnp.broadcast_to(part[None], (blocks, held_rows, width)),...  5.01 us
    unnamed x12, local copies, waits for them, and re-layouts  4.68 us
  transfers between devices with their start and end apart: 3, of which 3 were waited for; matrix products, arithmetic and copies ran while one was open for 2% of the time, Pallas kernels for 5%

profile of v4, /device:TPU:1, one launch (start us, length us, event | category | flops | bytes accessed | tf_op | source)
XLA Modules:
  0.0 99.5 jit_solution(14992723377602039766)
XLA Ops:
  0.6 0.0 copy-start
  0.7 0.9 copy-done
  1.6 0.7 broadcast_in_dim.15
  2.3 5.0 %all-to-all-start = ((bf16[4,72,384]{2,1,0:T(8,128)(2,1)}), bf16[4,72,384]{2,1,0:T(8,128)(2,1)S(1)}, u32[]{:S(2)}, u32[]{:S(2)}) async-start(bf16[4,72,384]{2,1,0:T(8,128)(2,1)} %broadcast_in_dim.15), calls=%async_computation | async-start | bytes 442368 | tf_op jit(solution)/shard_map/share_rows/all_to_all | solution.py:330
  7.3 0.7 convert_bitcast_fusion
  8.0 0.7 convert_bitcast_fusion.1
  8.6 0.7 pad_maximum_fusion.info_ref
  9.3 3.3 %all-to-all-done.rows_ref = bf16[4,72,384]{2,1,0:T(8,128)(2,1)S(1)} async-done(((bf16[4,72,384]{2,1,0:T(8,128)(2,1)}), bf16[4,72,384]{2,1,0:T(8,128)(2,1)S(1)}, u32[]{:S(2)}, u32[]{:S(2)}) %all-to-all-start) | async-done | bytes 221216 | tf_op jit(solution)/shard_map/share_rows/all_to_all | solution.py:330
  12.6 1.6 %line_sums.1 = s16[16,72,128]{2,1,0:T(8,128)(2,1)} custom-call(bf16[4,72,384]{2,1,0:T(8,128)(2,1)S(1)} %all-to-all-done.rows_ref, f32[6,128]{1,0:T(8,128)S(1)} %pad_maximum_fusion.info_ref), custom_call_target="tpu_custom_call" | custom-call | tf_op jit(solution)/shard_map/line_sums/pallas_call | solution.py:341
  14.1 14.9 %all-to-all-start.1 = ((s16[16,72,128]{2,1,0:T(8,128)(2,1)}), s16[16,72,128]{2,1,0:T(8,128)(2,1)S(1)}, u32[]{:S(2)}, u32[]{:S(2)}) async-start(s16[16,72,128]{2,1,0:T(8,128)(2,1)} %line_sums.1), calls=%async_computation.1 | async-start | bytes 589824 | tf_op jit(solution)/shard_map/share_sums/all_to_all | solution.py:351
  29.1 0.0 copy-start.1
  29.1 1.0 copy-done.1
  30.1 0.0 copy-start.2
  30.1 0.7 copy-done.2
  30.8 0.0 copy-start.3
  30.8 0.7 copy-done.3
  31.5 0.0 copy-start.4
  31.5 0.7 copy-done.4
  32.2 0.0 copy-start.5
  32.2 0.7 copy-done.5
  32.9 5.0 %prepare.1 = (bf16[8,1408,1408]{2,1,0:T(8,128)(2,1)}, f32[8,1408]{1,0:T(8,128)S(1)}, s32[24,128]{1,0:T(8,128)S(1)}, s16[16,128]{1,0:T(8,128)(2,1)S(1)}, bf16[128,1408]{1,0:T(8,128)(2,1)S(1)}) custom-call(f32[2,1326]{1,0:T(2,128)S(1)} %bitcast.11, s32[2,1326]{1,0:T(2,128)S(1)} %bitcast.12, s32[2,1326]{1,0:T(2,128)S(1)} %bitcast.13, s32[2,1326]{1,0:T(2,128)S(1)} %bitcast.14, ...), custom_call_target="tpu_custom_call" | custom-call | flops 31719424 | bytes 11894784 | tf_op jit(solution)/shard_map/prepare/pallas_call | solution.py:355
  37.9 4.3 %all-to-all-done.1.value_ref = s16[16,72,128]{2,1,0:T(8,128)(2,1)S(1)} async-done(((s16[16,72,128]{2,1,0:T(8,128)(2,1)}), s16[16,72,128]{2,1,0:T(8,128)(2,1)S(1)}, u32[]{:S(2)}, u32[]{:S(2)}) %all-to-all-start.1) | async-done | bytes 294944 | tf_op jit(solution)/shard_map/share_sums/all_to_all | solution.py:351
  42.2 9.5 %collective-permute-start = (s16[16,72,128]{2,1,0:T(8,128)(2,1)S(1)}, s16[16,72,128]{2,1,0:T(8,128)(2,1)S(1)}, u32[]{:S(2)}, u32[]{:S(2)}) collective-permute-start(s16[16,72,128]{2,1,0:T(8,128)(2,1)S(1)} %share_sums.1.mine_ref), channel_id=1, source_target_pairs={{0,64},{64,0},{128,192},{192,128},{256,320},{320,256},{384,448},{4... | collective-permute-start | bytes 884744 | tf_op jit(solution)/shard_map/share_sums/ppermute | solution.py:400
  51.7 1.2 %collective-permute-done.other_ref = s16[16,72,128]{2,1,0:T(8,128)(2,1)S(1)} collective-permute-done((s16[16,72,128]{2,1,0:T(8,128)(2,1)S(1)}, s16[16,72,128]{2,1,0:T(8,128)(2,1)S(1)}, u32[]{:S(2)}, u32[]{:S(2)}) %collective-permute-start) | collective-permute-done | bytes 294944 | tf_op jit(solution)/shard_map/share_sums/ppermute | solution.py:400
  52.9 6.8 %boards.1 = (f32[2,8,1326]{2,1,0:T(8,128)}, s16[16,8,1408]{2,1,0:T(8,128)(2,1)S(1)}) custom-call(s16[16,72,128]{2,1,0:T(8,128)(2,1)S(1)} %share_sums.1.mine_ref, s16[16,72,128]{2,1,0:T(8,128)(2,1)S(1)} %collective-permute-done.other_ref, f32[8,1408]{1,0:T(8,128)S(1)} %get-tuple-element.15.rows_ref, bf16[128,1408]{1,0:T(8,128)(2,1)S(1)} %get-tuple-element.16.cards_ref, ...), custom_call_target="tpu_custom_call" | custom-call | tf_op jit(solution)/shard_map/boards/pallas_call | solution.py:402
  59.6 21.4 %all_to_all.20.codes_ref = s16[16,8,1408]{2,1,0:T(8,128)(2,1)S(1)} all-to-all(s16[16,8,1408]{2,1,0:T(8,128)(2,1)S(1)} %get-tuple-element.20), channel_id=1, replica_groups=mesh['turn'=8,'river'=16,'bucket'=4] {'river'}, dimensions={0} | all-to-all | bytes 720896 | tf_op jit(solution)/shard_map/means/all_to_all | solution.py:425
  81.0 0.3 means.2
  81.3 17.4 %all_to_all.21.codes_ref = s16[8,8,1408]{2,1,0:T(8,128)(2,1)S(1)} all-to-all(s16[8,8,1408]{2,1,0:T(8,128)(2,1)S(1)} %get-tuple-element.21), channel_id=1, replica_groups=mesh['turn'=8,'river'=16,'bucket'=4] {'turn'}, dimensions={0} | all-to-all | bytes 360448 | tf_op jit(solution)/shard_map/means/all_to_all | solution.py:436
  98.7 0.7 means.3
  (2 shorter events, 0.0 us)
Async XLA Ops:
  0.6 0.9 copy-start
  2.3 10.3 %all-to-all-start = ((bf16[4,72,384]{2,1,0:T(8,128)(2,1)}), bf16[4,72,384]{2,1,0:T(8,128)(2,1)S(1)}, u32[]{:S(2)}, u32[]{:S(2)}) async-start(bf16[4,72,384]{2,1,0:T(8,128)(2,1)} %broadcast_in_dim.15), calls=%async_computation | async-start | bytes 442368 | tf_op jit(solution)/shard_map/share_rows/all_to_all | solution.py:330
  14.1 28.0 %all-to-all-start.1 = ((s16[16,72,128]{2,1,0:T(8,128)(2,1)}), s16[16,72,128]{2,1,0:T(8,128)(2,1)S(1)}, u32[]{:S(2)}, u32[]{:S(2)}) async-start(s16[16,72,128]{2,1,0:T(8,128)(2,1)} %line_sums.1), calls=%async_computation.1 | async-start | bytes 589824 | tf_op jit(solution)/shard_map/share_sums/all_to_all | solution.py:351
  29.1 1.0 copy-start.1
  30.1 0.7 copy-start.2
  30.8 0.7 copy-start.3
  31.5 0.7 copy-start.4
  32.2 0.7 copy-start.5
  42.2 10.7 %collective-permute-start = (s16[16,72,128]{2,1,0:T(8,128)(2,1)S(1)}, s16[16,72,128]{2,1,0:T(8,128)(2,1)S(1)}, u32[]{:S(2)}, u32[]{:S(2)}) collective-permute-start(s16[16,72,128]{2,1,0:T(8,128)(2,1)S(1)} %share_sums.1.mine_ref), channel_id=1, source_target_pairs={{0,64},{64,0},{128,192},{192,128},{256,320},{320,256},{384,448},{4... | collective-permute-start | bytes 884744 | tf_op jit(solution)/shard_map/share_sums/ppermute | solution.py:400

commit v5 on v4

--- a/solution.py
+++ b/solution.py
@@ -42,16 +42,24 @@
     return floor, code_scale(floor, most)
 
 
-def encode(x, floor, scale):
+def dither(rows, river):
+    row = lax.broadcasted_iota(jnp.int32, (rows, LANES), 0)
+    lane = lax.broadcasted_iota(jnp.int32, (rows, LANES), 1)
+    place = (row * 3091 + lane * 2333 + river * 1697) & 4095
+    return (place.astype(F32) + 0.5) * (1.0 / 4096)
+
+
+def encode(x, offset, floor, scale):
     size = jnp.log(1.0 + jnp.abs(x) * (1.0 / floor)) * (scale / np.log(2.0))
-    size = jnp.minimum(jnp.floor(size + 0.5), 32767.0)
+    size = jnp.minimum(jnp.floor(size + offset), 32767.0)
     return jnp.where(x < 0, -size, size).astype(jnp.int32).astype(I16)
 
 
-def decode(code, floor, scale):
+def decode(code, offset, floor, scale):
     code = code.astype(jnp.int32).astype(F32)
-    size = (jnp.exp(jnp.abs(code) * (np.log(2.0) / scale)) - 1.0) * floor
-    return jnp.where(code < 0, -size, size)
+    size = (jnp.abs(code) + (0.5 - offset)) * (np.log(2.0) / scale)
+    size = (jnp.exp(size) - 1.0) * floor
+    return jnp.where(code == 0, 0.0, jnp.where(code < 0, -size, size))
 
 
 def encode_rows(x, hands):
@@ -126,7 +134,7 @@
     for block in range(1, blocks):
         part = summed[block * rows : (block + 1) * rows]
         total += pltpu.roll(part, block * 2 * group, 1)
-    codes = encode(total, *code)
+    codes = encode(total, dither(rows, lax.axis_index("river")), *code)
     for copy in range(sums_ref.shape[0]):
         sums_ref[copy] = codes
 
@@ -219,10 +227,11 @@
         )
         contest_copies[board].start()
 
-    for part, ref in enumerate((mine_ref, other_ref)):
-        for river in range(rivers):
+    for river in range(rivers):
+        offset = dither(held_rows, river)
+        for part, ref in enumerate((mine_ref, other_ref)):
             at = (part * rivers + river) * held_rows
-            plain_ref[at : at + held_rows, :] = decode(ref[river], *in_code)
+            plain_ref[at : at + held_rows, :] = decode(ref[river], offset, *in_code)
     slots_copy.wait()
 
     for board in range(boards):

time: 100 us -> 100 us (level)
  no operation moved by 1% of the time
where the time goes in v5:
time: 100 us; the launch traced here: 99.5 us
  blocking collectives  38.8 us (39%)
  starting transfers between devices  29.4 us (29%)
  Pallas kernels  14.3 us (14%)
  waiting for transfers between devices  8.75 us (9%)
  local copies, waits for them, and re-layouts  5.4 us (5%)
  other arithmetic  2 us (2%)
    all_to_all x1, blocking collectives, local(): lax.all_to_all(partial, 'river', split_axis=0, concat_axis=0, tiled=True)  21.4 us
    all_to_all x1, blocking collectives, local(): lax.all_to_all(partial, 'turn', split_axis=0, concat_axis=0, tiled=True)  17.4 us
    all_to_all x1, starting transfers between devices, local(): lax.all_to_all(sums, 'river', split_axis=0, concat_axis=0, tiled=True)  14.9 us
    ppermute x1, starting transfers between devices, local(): other = lax.ppermute(mine, 'turn', swap)  9.52 us
    pallas_call x1, Pallas kernels, local(): pl.pallas_call(functools.partial(board_kernel, blocks, in_code), out_shap...  6.76 us
    pallas_call x1, Pallas kernels, local(): pl.pallas_call(functools.partial(prepare_kernel, shard_rows, held_rows, b...  5.03 us
    all_to_all x1, starting transfers between devices, local(): lax.all_to_all(jnp.broadcast_to(part[None], (blocks, held_rows, width)),...  5.01 us
    unnamed x12, local copies, waits for them, and re-layouts  4.68 us
  transfers between devices with their start and end apart: 3, of which 3 were waited for; matrix products, arithmetic and copies ran while one was open for 2% of the time, Pallas kernels for 5%

profile of v5, /device:TPU:1, one launch (start us, length us, event | category | flops | bytes accessed | tf_op | source)
XLA Modules:
  0.0 99.5 jit_solution(9121149937249438608)
XLA Ops:
  0.6 0.0 copy-start
  0.7 0.9 copy-done
  1.6 0.7 broadcast_in_dim.15
  2.3 5.0 %all-to-all-start = ((bf16[4,72,384]{2,1,0:T(8,128)(2,1)}), bf16[4,72,384]{2,1,0:T(8,128)(2,1)S(1)}, u32[]{:S(2)}, u32[]{:S(2)}) async-start(bf16[4,72,384]{2,1,0:T(8,128)(2,1)} %broadcast_in_dim.15), calls=%async_computation | async-start | bytes 442368 | tf_op jit(solution)/shard_map/share_rows/all_to_all | solution.py:339
  7.3 0.7 convert_bitcast_fusion
  8.0 0.7 convert_bitcast_fusion.1
  8.6 0.7 pad_maximum_fusion.info_ref
  9.3 3.3 %all-to-all-done.rows_ref = bf16[4,72,384]{2,1,0:T(8,128)(2,1)S(1)} async-done(((bf16[4,72,384]{2,1,0:T(8,128)(2,1)}), bf16[4,72,384]{2,1,0:T(8,128)(2,1)S(1)}, u32[]{:S(2)}, u32[]{:S(2)}) %all-to-all-start) | async-done | bytes 221216 | tf_op jit(solution)/shard_map/share_rows/all_to_all | solution.py:339
  12.6 1.6 %line_sums.1 = s16[16,72,128]{2,1,0:T(8,128)(2,1)} custom-call(bf16[4,72,384]{2,1,0:T(8,128)(2,1)S(1)} %all-to-all-done.rows_ref, f32[6,128]{1,0:T(8,128)S(1)} %pad_maximum_fusion.info_ref), custom_call_target="tpu_custom_call" | custom-call | tf_op jit(solution)/shard_map/line_sums/pallas_call | solution.py:350
  14.1 14.9 %all-to-all-start.1 = ((s16[16,72,128]{2,1,0:T(8,128)(2,1)}), s16[16,72,128]{2,1,0:T(8,128)(2,1)S(1)}, u32[]{:S(2)}, u32[]{:S(2)}) async-start(s16[16,72,128]{2,1,0:T(8,128)(2,1)} %line_sums.1), calls=%async_computation.1 | async-start | bytes 589824 | tf_op jit(solution)/shard_map/share_sums/all_to_all | solution.py:360
  29.1 0.0 copy-start.1
  29.1 1.0 copy-done.1
  30.1 0.0 copy-start.2
  30.1 0.7 copy-done.2
  30.8 0.0 copy-start.3
  30.8 0.7 copy-done.3
  31.5 0.0 copy-start.4
  31.5 0.7 copy-done.4
  32.2 0.0 copy-start.5
  32.2 0.7 copy-done.5
  32.9 5.0 %prepare.1 = (bf16[8,1408,1408]{2,1,0:T(8,128)(2,1)}, f32[8,1408]{1,0:T(8,128)S(1)}, s32[24,128]{1,0:T(8,128)S(1)}, s16[16,128]{1,0:T(8,128)(2,1)S(1)}, bf16[128,1408]{1,0:T(8,128)(2,1)S(1)}) custom-call(f32[2,1326]{1,0:T(2,128)S(1)} %bitcast.11, s32[2,1326]{1,0:T(2,128)S(1)} %bitcast.12, s32[2,1326]{1,0:T(2,128)S(1)} %bitcast.13, s32[2,1326]{1,0:T(2,128)S(1)} %bitcast.14, ...), custom_call_target="tpu_custom_call" | custom-call | flops 31719424 | bytes 11894784 | tf_op jit(solution)/shard_map/prepare/pallas_call | solution.py:364
  37.9 4.3 %all-to-all-done.1.value_ref = s16[16,72,128]{2,1,0:T(8,128)(2,1)S(1)} async-done(((s16[16,72,128]{2,1,0:T(8,128)(2,1)}), s16[16,72,128]{2,1,0:T(8,128)(2,1)S(1)}, u32[]{:S(2)}, u32[]{:S(2)}) %all-to-all-start.1) | async-done | bytes 294944 | tf_op jit(solution)/shard_map/share_sums/all_to_all | solution.py:360
  42.2 9.5 %collective-permute-start = (s16[16,72,128]{2,1,0:T(8,128)(2,1)S(1)}, s16[16,72,128]{2,1,0:T(8,128)(2,1)S(1)}, u32[]{:S(2)}, u32[]{:S(2)}) collective-permute-start(s16[16,72,128]{2,1,0:T(8,128)(2,1)S(1)} %share_sums.1.mine_ref), channel_id=1, source_target_pairs={{0,64},{64,0},{128,192},{192,128},{256,320},{320,256},{384,448},{4... | collective-permute-start | bytes 884744 | tf_op jit(solution)/shard_map/share_sums/ppermute | solution.py:409
  51.7 1.2 %collective-permute-done.other_ref = s16[16,72,128]{2,1,0:T(8,128)(2,1)S(1)} collective-permute-done((s16[16,72,128]{2,1,0:T(8,128)(2,1)S(1)}, s16[16,72,128]{2,1,0:T(8,128)(2,1)S(1)}, u32[]{:S(2)}, u32[]{:S(2)}) %collective-permute-start) | collective-permute-done | bytes 294944 | tf_op jit(solution)/shard_map/share_sums/ppermute | solution.py:409
  52.9 6.8 %boards.1 = (f32[2,8,1326]{2,1,0:T(8,128)}, s16[16,8,1408]{2,1,0:T(8,128)(2,1)S(1)}) custom-call(s16[16,72,128]{2,1,0:T(8,128)(2,1)S(1)} %share_sums.1.mine_ref, s16[16,72,128]{2,1,0:T(8,128)(2,1)S(1)} %collective-permute-done.other_ref, f32[8,1408]{1,0:T(8,128)S(1)} %get-tuple-element.15.rows_ref, bf16[128,1408]{1,0:T(8,128)(2,1)S(1)} %get-tuple-element.16.cards_ref, ...), custom_call_target="tpu_custom_call" | custom-call | tf_op jit(solution)/shard_map/boards/pallas_call | solution.py:411
  59.6 21.4 %all_to_all.20.codes_ref = s16[16,8,1408]{2,1,0:T(8,128)(2,1)S(1)} all-to-all(s16[16,8,1408]{2,1,0:T(8,128)(2,1)S(1)} %get-tuple-element.20), channel_id=1, replica_groups=mesh['turn'=8,'river'=16,'bucket'=4] {'river'}, dimensions={0} | all-to-all | bytes 720896 | tf_op jit(solution)/shard_map/means/all_to_all | solution.py:434
  81.0 0.3 means.2
  81.3 17.4 %all_to_all.21.codes_ref = s16[8,8,1408]{2,1,0:T(8,128)(2,1)S(1)} all-to-all(s16[8,8,1408]{2,1,0:T(8,128)(2,1)S(1)} %get-tuple-element.21), channel_id=1, replica_groups=mesh['turn'=8,'river'=16,'bucket'=4] {'turn'}, dimensions={0} | all-to-all | bytes 360448 | tf_op jit(solution)/shard_map/means/all_to_all | solution.py:445
  98.7 0.7 means.3
  (2 shorter events, 0.0 us)
Async XLA Ops:
  0.6 0.9 copy-start
  2.3 10.3 %all-to-all-start = ((bf16[4,72,384]{2,1,0:T(8,128)(2,1)}), bf16[4,72,384]{2,1,0:T(8,128)(2,1)S(1)}, u32[]{:S(2)}, u32[]{:S(2)}) async-start(bf16[4,72,384]{2,1,0:T(8,128)(2,1)} %broadcast_in_dim.15), calls=%async_computation | async-start | bytes 442368 | tf_op jit(solution)/shard_map/share_rows/all_to_all | solution.py:339
  14.1 28.0 %all-to-all-start.1 = ((s16[16,72,128]{2,1,0:T(8,128)(2,1)}), s16[16,72,128]{2,1,0:T(8,128)(2,1)S(1)}, u32[]{:S(2)}, u32[]{:S(2)}) async-start(s16[16,72,128]{2,1,0:T(8,128)(2,1)} %line_sums.1), calls=%async_computation.1 | async-start | bytes 589824 | tf_op jit(solution)/shard_map/share_sums/all_to_all | solution.py:360
  29.1 1.0 copy-start.1
  30.1 0.7 copy-start.2
  30.8 0.7 copy-start.3
  31.5 0.7 copy-start.4
  32.2 0.7 copy-start.5
  42.2 10.7 %collective-permute-start = (s16[16,72,128]{2,1,0:T(8,128)(2,1)S(1)}, s16[16,72,128]{2,1,0:T(8,128)(2,1)S(1)}, u32[]{:S(2)}, u32[]{:S(2)}) collective-permute-start(s16[16,72,128]{2,1,0:T(8,128)(2,1)S(1)} %share_sums.1.mine_ref), channel_id=1, source_target_pairs={{0,64},{64,0},{128,192},{192,128},{256,320},{320,256},{384,448},{4... | collective-permute-start | bytes 884744 | tf_op jit(solution)/shard_map/share_sums/ppermute | solution.py:409

commit v6 on v5

--- a/solution.py
+++ b/solution.py
@@ -234,34 +234,40 @@
             plain_ref[at : at + held_rows, :] = decode(ref[river], offset, *in_code)
     slots_copy.wait()
 
+    def place(board, chunk):
+        lanes = pl.ds(pl.multiple_of(chunk * LANES, LANES), LANES)
+        found = found_ref[lanes, :].T
+        group = rows_ref[board : board + 1, lanes]
+        reach = rows_ref[boards + board : boards + board + 1, lanes]
+        chosen = jnp.zeros((columns, LANES), F32)
+        for which in range(blocks):
+            chosen += jnp.where(
+                group == which, found[which * columns : (which + 1) * columns], 0.0
+            )
+        high, low = split_two(chosen * reach)
+        show_ref[board, 0:half, lanes] = high[0:half]
+        show_ref[board, half:columns, lanes] = low[0:half]
+        base = board * half
+        fold_ref[base : base + half, lanes] = high[half:columns]
+        base = (boards + board) * half
+        fold_ref[base : base + half, lanes] = low[half:columns]
+
+    def find(board, chunk):
+        base = pl.multiple_of(chunk * LANES, LANES)
+        for hand in range(LANES):
+            slot = slots_ref[board * chunks + chunk, hand]
+            found_ref[pl.ds(base + hand, 1), :] = plain_ref[pl.ds(slot, 1), :]
+
     for board in range(boards):
+        find(board, 0)
 
         def gather(chunk, carry, board=board):
-            base = pl.multiple_of(chunk * LANES, LANES)
-            for hand in range(LANES):
-                slot = slots_ref[board * chunks + chunk, hand]
-                found_ref[pl.ds(base + hand, 1), :] = plain_ref[pl.ds(slot, 1), :]
+            place(board, chunk - 1)
+            find(board, chunk)
             return carry
 
-        lax.fori_loop(0, chunks, gather, 0)
-
-        for chunk in range(chunks):
-            lanes = pl.ds(chunk * LANES, LANES)
-            found = found_ref[lanes, :].T
-            group = rows_ref[board : board + 1, lanes]
-            reach = rows_ref[boards + board : boards + board + 1, lanes]
-            chosen = jnp.zeros((columns, LANES), F32)
-            for which in range(blocks):
-                chosen += jnp.where(
-                    group == which, found[which * columns : (which + 1) * columns], 0.0
-                )
-            high, low = split_two(chosen * reach)
-            show_ref[board, 0:half, lanes] = high[0:half]
-            show_ref[board, half:columns, lanes] = low[0:half]
-            base = board * half
-            fold_ref[base : base + half, lanes] = high[half:columns]
-            base = (boards + board) * half
-            fold_ref[base : base + half, lanes] = low[half:columns]
+        lax.fori_loop(1, chunks, gather, 0)
+        place(board, chunks - 1)
 
     cards = cards_ref[...]
     folds = fold_ref[...]

time: 100 us -> 99.9 us (level)
  no operation moved by 1% of the time
where the time goes in v6:
time: 99.9 us; the launch traced here: 99.2 us
  blocking collectives  38.8 us (39%)
  starting transfers between devices  29.4 us (29%)
  Pallas kernels  14.1 us (14%)
  waiting for transfers between devices  8.75 us (9%)
  local copies, waits for them, and re-layouts  5.4 us (5%)
  other arithmetic  2 us (2%)
    all_to_all x1, blocking collectives, local(): lax.all_to_all(partial, 'river', split_axis=0, concat_axis=0, tiled=True)  21.4 us
    all_to_all x1, blocking collectives, local(): lax.all_to_all(partial, 'turn', split_axis=0, concat_axis=0, tiled=True)  17.4 us
    all_to_all x1, starting transfers between devices, local(): lax.all_to_all(sums, 'river', split_axis=0, concat_axis=0, tiled=True)  14.9 us
    ppermute x1, starting transfers between devices, local(): other = lax.ppermute(mine, 'turn', swap)  9.52 us
    pallas_call x1, Pallas kernels, local(): pl.pallas_call(functools.partial(board_kernel, blocks, in_code), out_shap...  6.53 us
    pallas_call x1, Pallas kernels, local(): pl.pallas_call(functools.partial(prepare_kernel, shard_rows, held_rows, b...  5.03 us
    all_to_all x1, starting transfers between devices, local(): lax.all_to_all(jnp.broadcast_to(part[None], (blocks, held_rows, width)),...  5.01 us
    unnamed x12, local copies, waits for them, and re-layouts  4.68 us
  transfers between devices with their start and end apart: 3, of which 3 were waited for; matrix products, arithmetic and copies ran while one was open for 2% of the time, Pallas kernels for 5%

profile of v6, /device:TPU:1, one launch (start us, length us, event | category | flops | bytes accessed | tf_op | source)
XLA Modules:
  0.0 99.2 jit_solution(13020419943747605400)
XLA Ops:
  0.6 0.0 copy-start
  0.7 0.9 copy-done
  1.6 0.7 broadcast_in_dim.15
  2.3 5.0 %all-to-all-start = ((bf16[4,72,384]{2,1,0:T(8,128)(2,1)}), bf16[4,72,384]{2,1,0:T(8,128)(2,1)S(1)}, u32[]{:S(2)}, u32[]{:S(2)}) async-start(bf16[4,72,384]{2,1,0:T(8,128)(2,1)} %broadcast_in_dim.15), calls=%async_computation | async-start | bytes 442368 | tf_op jit(solution)/shard_map/share_rows/all_to_all | solution.py:345
  7.3 0.7 convert_bitcast_fusion
  8.0 0.7 convert_bitcast_fusion.1
  8.6 0.7 pad_maximum_fusion.info_ref
  9.3 3.3 %all-to-all-done.rows_ref = bf16[4,72,384]{2,1,0:T(8,128)(2,1)S(1)} async-done(((bf16[4,72,384]{2,1,0:T(8,128)(2,1)}), bf16[4,72,384]{2,1,0:T(8,128)(2,1)S(1)}, u32[]{:S(2)}, u32[]{:S(2)}) %all-to-all-start) | async-done | bytes 221216 | tf_op jit(solution)/shard_map/share_rows/all_to_all | solution.py:345
  12.6 1.6 %line_sums.1 = s16[16,72,128]{2,1,0:T(8,128)(2,1)} custom-call(bf16[4,72,384]{2,1,0:T(8,128)(2,1)S(1)} %all-to-all-done.rows_ref, f32[6,128]{1,0:T(8,128)S(1)} %pad_maximum_fusion.info_ref), custom_call_target="tpu_custom_call" | custom-call | tf_op jit(solution)/shard_map/line_sums/pallas_call | solution.py:356
  14.1 14.9 %all-to-all-start.1 = ((s16[16,72,128]{2,1,0:T(8,128)(2,1)}), s16[16,72,128]{2,1,0:T(8,128)(2,1)S(1)}, u32[]{:S(2)}, u32[]{:S(2)}) async-start(s16[16,72,128]{2,1,0:T(8,128)(2,1)} %line_sums.1), calls=%async_computation.1 | async-start | bytes 589824 | tf_op jit(solution)/shard_map/share_sums/all_to_all | solution.py:366
  29.1 0.0 copy-start.1
  29.1 1.0 copy-done.1
  30.1 0.0 copy-start.2
  30.1 0.7 copy-done.2
  30.8 0.0 copy-start.3
  30.8 0.7 copy-done.3
  31.5 0.0 copy-start.4
  31.5 0.7 copy-done.4
  32.2 0.0 copy-start.5
  32.2 0.7 copy-done.5
  32.9 5.0 %prepare.1 = (bf16[8,1408,1408]{2,1,0:T(8,128)(2,1)}, f32[8,1408]{1,0:T(8,128)S(1)}, s32[24,128]{1,0:T(8,128)S(1)}, s16[16,128]{1,0:T(8,128)(2,1)S(1)}, bf16[128,1408]{1,0:T(8,128)(2,1)S(1)}) custom-call(f32[2,1326]{1,0:T(2,128)S(1)} %bitcast.11, s32[2,1326]{1,0:T(2,128)S(1)} %bitcast.12, s32[2,1326]{1,0:T(2,128)S(1)} %bitcast.13, s32[2,1326]{1,0:T(2,128)S(1)} %bitcast.14, ...), custom_call_target="tpu_custom_call" | custom-call | flops 31719424 | bytes 11894784 | tf_op jit(solution)/shard_map/prepare/pallas_call | solution.py:370
  37.9 4.3 %all-to-all-done.1.value_ref = s16[16,72,128]{2,1,0:T(8,128)(2,1)S(1)} async-done(((s16[16,72,128]{2,1,0:T(8,128)(2,1)}), s16[16,72,128]{2,1,0:T(8,128)(2,1)S(1)}, u32[]{:S(2)}, u32[]{:S(2)}) %all-to-all-start.1) | async-done | bytes 294944 | tf_op jit(solution)/shard_map/share_sums/all_to_all | solution.py:366
  42.2 9.5 %collective-permute-start = (s16[16,72,128]{2,1,0:T(8,128)(2,1)S(1)}, s16[16,72,128]{2,1,0:T(8,128)(2,1)S(1)}, u32[]{:S(2)}, u32[]{:S(2)}) collective-permute-start(s16[16,72,128]{2,1,0:T(8,128)(2,1)S(1)} %share_sums.1.mine_ref), channel_id=1, source_target_pairs={{0,64},{64,0},{128,192},{192,128},{256,320},{320,256},{384,448},{4... | collective-permute-start | bytes 884744 | tf_op jit(solution)/shard_map/share_sums/ppermute | solution.py:415
  51.7 1.2 %collective-permute-done.other_ref = s16[16,72,128]{2,1,0:T(8,128)(2,1)S(1)} collective-permute-done((s16[16,72,128]{2,1,0:T(8,128)(2,1)S(1)}, s16[16,72,128]{2,1,0:T(8,128)(2,1)S(1)}, u32[]{:S(2)}, u32[]{:S(2)}) %collective-permute-start) | collective-permute-done | bytes 294944 | tf_op jit(solution)/shard_map/share_sums/ppermute | solution.py:415
  52.9 6.5 %boards.1 = (f32[2,8,1326]{2,1,0:T(8,128)}, s16[16,8,1408]{2,1,0:T(8,128)(2,1)S(1)}) custom-call(s16[16,72,128]{2,1,0:T(8,128)(2,1)S(1)} %share_sums.1.mine_ref, s16[16,72,128]{2,1,0:T(8,128)(2,1)S(1)} %collective-permute-done.other_ref, f32[8,1408]{1,0:T(8,128)S(1)} %get-tuple-element.15.rows_ref, bf16[128,1408]{1,0:T(8,128)(2,1)S(1)} %get-tuple-element.16.cards_ref, ...), custom_call_target="tpu_custom_call" | custom-call | tf_op jit(solution)/shard_map/boards/pallas_call | solution.py:417
  59.4 21.4 %all_to_all.20.codes_ref = s16[16,8,1408]{2,1,0:T(8,128)(2,1)S(1)} all-to-all(s16[16,8,1408]{2,1,0:T(8,128)(2,1)S(1)} %get-tuple-element.20), channel_id=1, replica_groups=mesh['turn'=8,'river'=16,'bucket'=4] {'river'}, dimensions={0} | all-to-all | bytes 720896 | tf_op jit(solution)/shard_map/means/all_to_all | solution.py:440
  80.8 0.3 means.2
  81.1 17.4 %all_to_all.21.codes_ref = s16[8,8,1408]{2,1,0:T(8,128)(2,1)S(1)} all-to-all(s16[8,8,1408]{2,1,0:T(8,128)(2,1)S(1)} %get-tuple-element.21), channel_id=1, replica_groups=mesh['turn'=8,'river'=16,'bucket'=4] {'turn'}, dimensions={0} | all-to-all | bytes 360448 | tf_op jit(solution)/shard_map/means/all_to_all | solution.py:451
  98.5 0.7 means.3
  (2 shorter events, 0.0 us)
Async XLA Ops:
  0.6 0.9 copy-start
  2.3 10.3 %all-to-all-start = ((bf16[4,72,384]{2,1,0:T(8,128)(2,1)}), bf16[4,72,384]{2,1,0:T(8,128)(2,1)S(1)}, u32[]{:S(2)}, u32[]{:S(2)}) async-start(bf16[4,72,384]{2,1,0:T(8,128)(2,1)} %broadcast_in_dim.15), calls=%async_computation | async-start | bytes 442368 | tf_op jit(solution)/shard_map/share_rows/all_to_all | solution.py:345
  14.1 28.0 %all-to-all-start.1 = ((s16[16,72,128]{2,1,0:T(8,128)(2,1)}), s16[16,72,128]{2,1,0:T(8,128)(2,1)S(1)}, u32[]{:S(2)}, u32[]{:S(2)}) async-start(s16[16,72,128]{2,1,0:T(8,128)(2,1)} %line_sums.1), calls=%async_computation.1 | async-start | bytes 589824 | tf_op jit(solution)/shard_map/share_sums/all_to_all | solution.py:366
  29.1 1.0 copy-start.1
  30.1 0.7 copy-start.2
  30.8 0.7 copy-start.3
  31.5 0.7 copy-start.4
  32.2 0.7 copy-start.5
  42.2 10.7 %collective-permute-start = (s16[16,72,128]{2,1,0:T(8,128)(2,1)S(1)}, s16[16,72,128]{2,1,0:T(8,128)(2,1)S(1)}, u32[]{:S(2)}, u32[]{:S(2)}) collective-permute-start(s16[16,72,128]{2,1,0:T(8,128)(2,1)S(1)} %share_sums.1.mine_ref), channel_id=1, source_target_pairs={{0,64},{64,0},{128,192},{192,128},{256,320},{320,256},{384,448},{4... | collective-permute-start | bytes 884744 | tf_op jit(solution)/shard_map/share_sums/ppermute | solution.py:415

commit v7 on v6

--- a/solution.py
+++ b/solution.py
@@ -14,7 +14,7 @@
 CARDS = 52
 TILE = 16
 CORES = 2
-CONTEST_PLACES = 8
+CONTEST_PLACES = 16
 SMALL = 8 * 2**20
 F32 = jnp.float32
 BF16 = jnp.bfloat16
@@ -190,7 +190,7 @@
         for board in range(boards):
             order = rank_rows[board : board + 1, :] - ranks[:, board : board + 1]
             contest = jnp.where(shared == 0.0, jnp.clip(order, -1.0, 1.0), 0.0)
-            contest_ref[board, lines, :] = contest.astype(BF16)
+            contest_ref[board, lines, :] = contest.astype(jnp.int32).astype(jnp.int8)
         copy = pltpu.make_async_copy(
             contest_ref.at[:, lines, :], contest_hbm.at[0:boards, lines, :], sems.at[chunk]
         )
@@ -285,7 +285,9 @@
     river_copies = []
     for board in range(boards):
         contest_copies[board].wait()
-        shown = jnp.dot(show_ref[board], contest_ref[board], preferred_element_type=F32)
+        shown = jnp.dot(
+            show_ref[board], contest_ref[board].astype(BF16), preferred_element_type=F32
+        )
         value = shown[0:half] + shown[half:columns] + folded[board * half : (board + 1) * half]
         best = jnp.maximum(value[0:entries], value[entries:half])
         best = best * rows_ref[2 * boards + board : 2 * boards + board + 1, :]
@@ -370,7 +372,7 @@
         contest, hand_rows, slots, token, cards = pl.pallas_call(
             functools.partial(prepare_kernel, shard_rows, held_rows, blocks, rivers),
             out_shape=(
-                jax.ShapeDtypeStruct((CONTEST_PLACES, padded, padded), BF16),
+                jax.ShapeDtypeStruct((CONTEST_PLACES, padded, padded), jnp.int8),
                 jax.ShapeDtypeStruct((8, padded), F32),
                 jax.ShapeDtypeStruct(slot_shape, jnp.int32),
                 jax.ShapeDtypeStruct((16, LANES), I16),
@@ -385,7 +387,7 @@
                 pltpu.VMEM((boards, hands), jnp.int32),
                 pltpu.VMEM((boards, padded), F32),
                 pltpu.VMEM((LANES, padded), F32),
-                pltpu.VMEM((boards, padded, padded), BF16),
+                pltpu.VMEM((boards, padded, padded), jnp.int8),
                 pltpu.SemaphoreType.DMA((5,)),
                 pltpu.SemaphoreType.DMA((chunks,)),
             ],
@@ -423,7 +425,7 @@
             in_specs=[whole_vmem()] * 4 + [pl.BlockSpec(memory_space=pl.ANY)] * 2,
             out_specs=(pl.BlockSpec(memory_space=pl.ANY), whole_vmem()),
             scratch_shapes=[
-                pltpu.VMEM((boards, padded, padded), BF16),
+                pltpu.VMEM((boards, padded, padded), jnp.int8),
                 pltpu.SMEM(slots.shape, jnp.int32),
                 pltpu.VMEM((CORES * rivers * held_rows, LANES), F32),
                 pltpu.VMEM((padded, LANES), F32),

time: 99.9 us -> 99.9 us (level)
  no operation moved by 1% of the time
where the time goes in v7:
time: 99.9 us; the launch traced here: 99.2 us
  blocking collectives  38.8 us (39%)
  starting transfers between devices  29.4 us (29%)
  Pallas kernels  14.3 us (14%)
  waiting for transfers between devices  8.54 us (9%)
  local copies, waits for them, and re-layouts  5.4 us (5%)
  other arithmetic  2 us (2%)
    all_to_all x1, blocking collectives, local(): lax.all_to_all(partial, 'river', split_axis=0, concat_axis=0, tiled=True)  21.4 us
    all_to_all x1, blocking collectives, local(): lax.all_to_all(partial, 'turn', split_axis=0, concat_axis=0, tiled=True)  17.4 us
    all_to_all x1, starting transfers between devices, local(): lax.all_to_all(sums, 'river', split_axis=0, concat_axis=0, tiled=True)  14.9 us
    ppermute x1, starting transfers between devices, local(): other = lax.ppermute(mine, 'turn', swap)  9.52 us
    pallas_call x1, Pallas kernels, local(): pl.pallas_call(functools.partial(board_kernel, blocks, in_code), out_shap...  6.54 us
    pallas_call x1, Pallas kernels, local(): pl.pallas_call(functools.partial(prepare_kernel, shard_rows, held_rows, b...  5.23 us
    all_to_all x1, starting transfers between devices, local(): lax.all_to_all(jnp.broadcast_to(part[None], (blocks, held_rows, width)),...  5.01 us
    unnamed x12, local copies, waits for them, and re-layouts  4.68 us
  transfers between devices with their start and end apart: 3, of which 3 were waited for; matrix products, arithmetic and copies ran while one was open for 2% of the time, Pallas kernels for 5%

profile of v7, /device:TPU:1, one launch (start us, length us, event | category | flops | bytes accessed | tf_op | source)
XLA Modules:
  0.0 99.2 jit_solution(13431637536947894862)
XLA Ops:
  0.6 0.0 copy-start
  0.7 0.9 copy-done
  1.6 0.7 broadcast_in_dim.15
  2.3 5.0 %all-to-all-start = ((bf16[4,72,384]{2,1,0:T(8,128)(2,1)}), bf16[4,72,384]{2,1,0:T(8,128)(2,1)S(1)}, u32[]{:S(2)}, u32[]{:S(2)}) async-start(bf16[4,72,384]{2,1,0:T(8,128)(2,1)} %broadcast_in_dim.15), calls=%async_computation | async-start | bytes 442368 | tf_op jit(solution)/shard_map/share_rows/all_to_all | solution.py:347
  7.3 0.7 convert_bitcast_fusion
  8.0 0.7 convert_bitcast_fusion.1
  8.6 0.7 pad_maximum_fusion.info_ref
  9.3 3.3 %all-to-all-done.rows_ref = bf16[4,72,384]{2,1,0:T(8,128)(2,1)S(1)} async-done(((bf16[4,72,384]{2,1,0:T(8,128)(2,1)}), bf16[4,72,384]{2,1,0:T(8,128)(2,1)S(1)}, u32[]{:S(2)}, u32[]{:S(2)}) %all-to-all-start) | async-done | bytes 221216 | tf_op jit(solution)/shard_map/share_rows/all_to_all | solution.py:347
  12.6 1.6 %line_sums.1 = s16[16,72,128]{2,1,0:T(8,128)(2,1)} custom-call(bf16[4,72,384]{2,1,0:T(8,128)(2,1)S(1)} %all-to-all-done.rows_ref, f32[6,128]{1,0:T(8,128)S(1)} %pad_maximum_fusion.info_ref), custom_call_target="tpu_custom_call" | custom-call | tf_op jit(solution)/shard_map/line_sums/pallas_call | solution.py:358
  14.1 14.9 %all-to-all-start.1 = ((s16[16,72,128]{2,1,0:T(8,128)(2,1)}), s16[16,72,128]{2,1,0:T(8,128)(2,1)S(1)}, u32[]{:S(2)}, u32[]{:S(2)}) async-start(s16[16,72,128]{2,1,0:T(8,128)(2,1)} %line_sums.1), calls=%async_computation.1 | async-start | bytes 589824 | tf_op jit(solution)/shard_map/share_sums/all_to_all | solution.py:368
  29.1 0.0 copy-start.1
  29.1 1.0 copy-done.1
  30.1 0.0 copy-start.2
  30.1 0.7 copy-done.2
  30.8 0.0 copy-start.3
  30.8 0.7 copy-done.3
  31.5 0.0 copy-start.4
  31.5 0.7 copy-done.4
  32.2 0.0 copy-start.5
  32.2 0.7 copy-done.5
  32.9 5.2 %prepare.1 = (s8[16,1408,1408]{2,1,0:T(32,128)(4,1)}, f32[8,1408]{1,0:T(8,128)S(1)}, s32[24,128]{1,0:T(8,128)S(1)}, s16[16,128]{1,0:T(8,128)(2,1)S(1)}, bf16[128,1408]{1,0:T(8,128)(2,1)S(1)}) custom-call(f32[2,1326]{1,0:T(2,128)S(1)} %bitcast.11, s32[2,1326]{1,0:T(2,128)S(1)} %bitcast.12, s32[2,1326]{1,0:T(2,128)S(1)} %bitcast.13, s32[2,1326]{1,0:T(2,128)S(1)} %bitcast.14, ...), custom_call_target="tpu_custom_call" | custom-call | flops 31719424 | bytes 11894784 | tf_op jit(solution)/shard_map/prepare/pallas_call | solution.py:372
  38.1 4.1 %all-to-all-done.1.value_ref = s16[16,72,128]{2,1,0:T(8,128)(2,1)S(1)} async-done(((s16[16,72,128]{2,1,0:T(8,128)(2,1)}), s16[16,72,128]{2,1,0:T(8,128)(2,1)S(1)}, u32[]{:S(2)}, u32[]{:S(2)}) %all-to-all-start.1) | async-done | bytes 294944 | tf_op jit(solution)/shard_map/share_sums/all_to_all | solution.py:368
  42.2 9.5 %collective-permute-start = (s16[16,72,128]{2,1,0:T(8,128)(2,1)S(1)}, s16[16,72,128]{2,1,0:T(8,128)(2,1)S(1)}, u32[]{:S(2)}, u32[]{:S(2)}) collective-permute-start(s16[16,72,128]{2,1,0:T(8,128)(2,1)S(1)} %share_sums.1.mine_ref), channel_id=1, source_target_pairs={{0,64},{64,0},{128,192},{192,128},{256,320},{320,256},{384,448},{4... | collective-permute-start | bytes 884744 | tf_op jit(solution)/shard_map/share_sums/ppermute | solution.py:417
  51.7 1.2 %collective-permute-done.other_ref = s16[16,72,128]{2,1,0:T(8,128)(2,1)S(1)} collective-permute-done((s16[16,72,128]{2,1,0:T(8,128)(2,1)S(1)}, s16[16,72,128]{2,1,0:T(8,128)(2,1)S(1)}, u32[]{:S(2)}, u32[]{:S(2)}) %collective-permute-start) | collective-permute-done | bytes 294944 | tf_op jit(solution)/shard_map/share_sums/ppermute | solution.py:417
  52.9 6.5 %boards.1 = (f32[2,8,1326]{2,1,0:T(8,128)}, s16[16,8,1408]{2,1,0:T(8,128)(2,1)S(1)}) custom-call(s16[16,72,128]{2,1,0:T(8,128)(2,1)S(1)} %share_sums.1.mine_ref, s16[16,72,128]{2,1,0:T(8,128)(2,1)S(1)} %collective-permute-done.other_ref, f32[8,1408]{1,0:T(8,128)S(1)} %get-tuple-element.15.rows_ref, bf16[128,1408]{1,0:T(8,128)(2,1)S(1)} %get-tuple-element.16.cards_ref, ...), custom_call_target="tpu_custom_call" | custom-call | tf_op jit(solution)/shard_map/boards/pallas_call | solution.py:419
  59.4 21.4 %all_to_all.20.codes_ref = s16[16,8,1408]{2,1,0:T(8,128)(2,1)S(1)} all-to-all(s16[16,8,1408]{2,1,0:T(8,128)(2,1)S(1)} %get-tuple-element.20), channel_id=1, replica_groups=mesh['turn'=8,'river'=16,'bucket'=4] {'river'}, dimensions={0} | all-to-all | bytes 720896 | tf_op jit(solution)/shard_map/means/all_to_all | solution.py:442
  80.8 0.3 means.2
  81.1 17.4 %all_to_all.21.codes_ref = s16[8,8,1408]{2,1,0:T(8,128)(2,1)S(1)} all-to-all(s16[8,8,1408]{2,1,0:T(8,128)(2,1)S(1)} %get-tuple-element.21), channel_id=1, replica_groups=mesh['turn'=8,'river'=16,'bucket'=4] {'turn'}, dimensions={0} | all-to-all | bytes 360448 | tf_op jit(solution)/shard_map/means/all_to_all | solution.py:453
  98.5 0.7 means.3
  (2 shorter events, 0.0 us)
Async XLA Ops:
  0.6 0.9 copy-start
  2.3 10.3 %all-to-all-start = ((bf16[4,72,384]{2,1,0:T(8,128)(2,1)}), bf16[4,72,384]{2,1,0:T(8,128)(2,1)S(1)}, u32[]{:S(2)}, u32[]{:S(2)}) async-start(bf16[4,72,384]{2,1,0:T(8,128)(2,1)} %broadcast_in_dim.15), calls=%async_computation | async-start | bytes 442368 | tf_op jit(solution)/shard_map/share_rows/all_to_all | solution.py:347
  14.1 28.0 %all-to-all-start.1 = ((s16[16,72,128]{2,1,0:T(8,128)(2,1)}), s16[16,72,128]{2,1,0:T(8,128)(2,1)S(1)}, u32[]{:S(2)}, u32[]{:S(2)}) async-start(s16[16,72,128]{2,1,0:T(8,128)(2,1)} %line_sums.1), calls=%async_computation.1 | async-start | bytes 589824 | tf_op jit(solution)/shard_map/share_sums/all_to_all | solution.py:368
  29.1 1.0 copy-start.1
  30.1 0.7 copy-start.2
  30.8 0.7 copy-start.3
  31.5 0.7 copy-start.4
  32.2 0.7 copy-start.5
  42.2 10.7 %collective-permute-start = (s16[16,72,128]{2,1,0:T(8,128)(2,1)S(1)}, s16[16,72,128]{2,1,0:T(8,128)(2,1)S(1)}, u32[]{:S(2)}, u32[]{:S(2)}) collective-permute-start(s16[16,72,128]{2,1,0:T(8,128)(2,1)S(1)} %share_sums.1.mine_ref), channel_id=1, source_target_pairs={{0,64},{64,0},{128,192},{192,128},{256,320},{320,256},{384,448},{4... | collective-permute-start | bytes 884744 | tf_op jit(solution)/shard_map/share_sums/ppermute | solution.py:417
